TPU v7x, 512 devices: a whole 4x8x8 slice. The times are simulated.
512 devices in a mesh: grp: 32 (over x, y), tp: 16 (over z, core).
Axes of the slice: x: 4, y: 8, z: 8, core: 2. Of those that a mesh axis runs over, the one named last changes fastest.
Arguments:
- activations: bfloat16 [8192, 8192], P('grp', 'tp'), may hold values from -6 to 6
- kv_weight: bfloat16 [8192, 2048], P(None, 'tp'), may hold values from -0.0625 to 0.0625
- store_down: bfloat16 [32, 8192, 128], P(None, ('tp', 'grp')), may hold values from -0.0625 to 0.0625
- store_up: bfloat16 [32, 128, 2048], P(None, 'grp', 'tp'), may hold values from -0.375 to 0.375
- block_home: int32 [32], replicated, may hold values from 0 to 31, each once
- group_variants: int32 [32, 4], replicated, may hold values from 0 to 15, as said below
- row_variant: int32 [8192, 1], P('grp'), may hold values from 0 to 3; in each aligned block of 256 rows (0 to 255, 256 to 511, ...) at most 192 rows name the same one
Outputs:
- kv_out: bfloat16 [8192, 2048], P('grp', 'tp')
Inputs may be any that keep to these rules, and one draw needn't show every extreme that they name: `group_variants`: each row lists 4 different variants; every variant is listed by some group. `row_variant`: among the tokens of one group no position is named by more than 192 tokens.
All inputs are finite; a program needn't handle non-finite values.
Results may differ from a plain program's by a relative error of at most 0.014.
Values may be sent and summed in bfloat16 or wider, within the bound.
A program may use at most 64 MiB of HBM per device.

v0:
```python
import jax
import jax.numpy as jnp
from jax import lax
from jax.sharding import PartitionSpec as P

PIECES = 2
VPG = 4
CAP = 192


def on_device(
    activations, kv_weight, store_down, store_up, block_home, group_variants, row_variant
):
    tokens = activations.shape[0]
    width_part = kv_weight.shape[1]
    group_index = lax.axis_index("grp")
    offsets = jnp.arange(PIECES, dtype=jnp.int32)
    slots_all = block_home[group_variants[:, :, None] * PIECES + offsets[None, None, :]]
    slots_all = slots_all.reshape(group_variants.shape[0], VPG * PIECES)
    slots_mine = lax.dynamic_index_in_dim(slots_all, group_index, 0, keepdims=False)
    whole_down, whole_up = (
        lax.all_gather(store_down, "grp", axis=1, tiled=True),
        lax.all_gather(store_up, "grp", axis=1, tiled=True),
    )
    need_down = whole_down[slots_mine]
    need_up = whole_up[slots_mine]
    variant_col = row_variant[:, 0]
    one_hot = (variant_col[:, None] == jnp.arange(VPG, dtype=jnp.int32)[None, :]).astype(jnp.int32)
    earlier = jnp.cumsum(one_hot, axis=0) - one_hot
    position = jnp.sum(earlier * one_hot, axis=1)
    slot_index = variant_col * CAP + position
    source_row = (
        jnp.zeros((VPG * CAP,), jnp.int32).at[slot_index].set(jnp.arange(tokens, dtype=jnp.int32))
    )
    counts = jnp.sum(one_hot, axis=0)
    filled = (jnp.arange(CAP, dtype=jnp.int32)[None, :] < counts[:, None]).reshape(VPG * CAP)
    grouped = jnp.where(filled[:, None], activations[source_row], jnp.zeros((), jnp.bfloat16))
    grouped = grouped.reshape(VPG, CAP, activations.shape[1])
    down_blocks = need_down.reshape(VPG, PIECES, need_down.shape[1], need_down.shape[2])
    partial_rank = jnp.einsum(
        "vcd,vpdr->vcpr", grouped, down_blocks, preferred_element_type=jnp.float32
    )
    rank_width = PIECES * need_down.shape[2]
    partial_rank = partial_rank.reshape(VPG, CAP, rank_width)
    base_out = jnp.dot(
        lax.all_gather(activations, "tp", axis=1, tiled=True),
        kv_weight,
        preferred_element_type=jnp.float32,
    )
    shrunk = lax.psum(partial_rank, "tp")
    shrunk_bf = shrunk.astype(jnp.bfloat16)
    up_blocks = need_up.reshape(VPG, PIECES * need_up.shape[1], need_up.shape[2])
    expanded = jnp.einsum("vcr,vrk->vck", shrunk_bf, up_blocks, preferred_element_type=jnp.float32)
    delta_rows = expanded.reshape(VPG * CAP, width_part)[slot_index]
    return (base_out + delta_rows).astype(jnp.bfloat16)


def solution(mesh):
    in_specs = (
        P("grp", "tp"),
        P(None, "tp"),
        P(None, ("tp", "grp"), None),
        P(None, "grp", "tp"),
        P(),
        P(),
        P("grp", None),
    )
    out_specs = P("grp", "tp")
    return jax.shard_map(
        on_device, mesh=mesh, in_specs=in_specs, out_specs=out_specs, check_vma=False
    )
```

profile of v0, /device:TPU:1, one launch (start us, length us, event | category | flops | bytes accessed | tf_op | source)
XLA Modules:
  0.0 260.2 jit_solution(6581367962212678838)
XLA Ops:
  6.5 1.5 copy.24
  8.1 0.0 all-gather.8.cloned.1.call-update
  8.1 0.0 all-gather.6.cloned.1.call-start
  8.2 0.7 all-gather.6.cloned.1.call-update
  8.9 0.0 all-gather.4.cloned.1.call-start
  8.9 0.7 all-gather.4.cloned.1.call-update
  9.6 0.7 broadcast_multiply_fusion
  10.3 0.1 copy.22
  10.4 0.1 compare_select_fusion
  10.5 0.1 reshape.112
  10.7 1.9 gather_fusion.1
  12.5 0.1 reshape.97
  12.7 1.2 reduce-window.6
  13.9 0.1 slice.18
  14.0 0.1 copy.20
  14.1 0.1 copy.21
  14.2 0.1 add_bitcast_fusion
  14.3 0.1 convert_reduce_fusion
  14.4 1.4 scatter_custom_fusion
  15.9 3.3 %gather_fusion = bf16[768,512]{1,0:T(8,128)(2,1)} fusion(bf16[256,512]{1,0:T(8,128)(2,1)S(1)} %copy-done.2, s32[1024]{0:T(1024)S(1)} %pad_clamp_fusion.3), kind=kCustom, calls=%fused_computation | custom fusion | bytes 1575936 | tf_op jit(solution)/shard_map/gather | solution.py:37
  19.2 0.1 iota_compare_fusion.1
  19.3 73.8 %all-gather.8.cloned.1.call-done = bf16[32,128,128]{2,0,1:T(8,128)(2,1)} async-done(((bf16[32,4,128]{2,0,1:T(8,128)(2,1)}), bf16[32,128,128]{2,0,1:T(8,128)(2,1)}) %all-gather.8.cloned.1.call-update) | async-done | bytes 1048592 | tf_op jit(solution)/shard_map/all_gather | solution.py:23
  93.1 1.6 copy.25
  94.7 0.6 gather_fusion.3
  95.3 88.4 %all-gather.6.cloned.1.call-done = bf16[32,512,128]{2,1,0:T(8,128)(2,1)} async-done(((bf16[32,16,128]{2,1,0:T(8,128)(2,1)}), bf16[32,512,128]{2,1,0:T(8,128)(2,1)}) %all-gather.6.cloned.1.call-update) | async-done | bytes 4194320 | tf_op jit(solution)/shard_map/all_gather | solution.py:22
  183.7 2.9 %gather_fusion.2 = bf16[8,512,128]{2,1,0:T(8,128)(2,1)S(1)} fusion(bf16[32,512,128]{2,1,0:T(8,128)(2,1)} %all-gather.6.cloned.1.call-done, s32[1024]{0:T(1024)S(1)} %pad_clamp_fusion.1), kind=kCustom, calls=%fused_computation.2 | custom fusion | bytes 2097184 | tf_op jit(solution)/shard_map/gather | solution.py:25
  186.7 1.5 convolution_bitcast_fusion
  188.2 0.1 copy.31
  188.3 60.3 %all-reduce.1 = bf16[4,192,256]{2,1,0:T(8,128)(2,1)S(1)} all-reduce(f32[4,192,256]{2,1,0:T(8,128)S(1)} %bitcast.41), channel_id=1, replica_groups=mesh['grp'=32,'tp'=16] {'tp'}, use_global_device_ids=true, to_apply=%region_5.6 | all-reduce | flops 196608 | bytes 1179648 | tf_op jit(solution)/shard_map/psum | solution.py:50
  248.6 0.2 fusion.13
  248.9 0.7 gather_fusion.4
  249.6 4.1 %fusion = bf16[256,128]{1,0:T(8,128)(2,1)} fusion(f32[256,128]{1,0:T(8,128)S(1)} %gather_fusion.4, bf16[256,8192]{1,0:T(8,128)(2,1)} %all-gather.4.cloned.1.call-done, bf16[8192,128]{1,0:T(8,128)(2,1)S(1)} %copy-done), kind=kOutput, calls=%fused_computation.8 | convolution fusion | flops 536936448 | bytes 6488064 | tf_op jit(solution)/shard_map/dot_general | solution.py:45
  (21 shorter events, 0.1 us)
Async XLA Ops:
  6.5 243.1 %copy-start = (bf16[8192,128]{1,0:T(8,128)(2,1)S(1)}, bf16[8192,128]{1,0:T(8,128)(2,1)}, u32[]{:S(2)}) copy-start(bf16[8192,128]{1,0:T(8,128)(2,1)} %param.8) | copy-start | bytes 6291460
  6.5 4.1 %copy-start.1 = (s32[32]{0:T(128)S(1)}, s32[32]{0:T(128)}, u32[]{:S(2)}) copy-start(s32[32]{0:T(128)} %param.11) | copy-start | bytes 388
  6.5 86.5 %all-gather.8.cloned.1.call-start = ((), (), s32[]{:S(2)}) async-start(), calls=%async_computation.2 | async-start | bytes 1081344 | tf_op jit(solution)/shard_map/all_gather | solution.py:23
  8.1 175.6 %all-gather.6.cloned.1.call-start = ((), (), s32[]{:S(2)}) async-start(), calls=%async_computation.1 | async-start | bytes 4325376 | tf_op jit(solution)/shard_map/all_gather | solution.py:22
  8.9 240.8 %all-gather.4.cloned.1.call-start = ((), (), s32[]{:S(2)}) async-start(), calls=%async_computation | async-start | bytes 4456448 | tf_op jit(solution)/shard_map/all_gather | solution.py:46
  10.7 2.0 copy-start.3
  10.7 5.2 %copy-start.2 = (bf16[256,512]{1,0:T(8,128)(2,1)S(1)}, bf16[256,512]{1,0:T(8,128)(2,1)}, u32[]{:S(2)}) copy-start(bf16[256,512]{1,0:T(8,128)(2,1)} %param.7) | copy-start | bytes 786436
Sparse Core Ops, SparseCore 0:
  10.5 82.4 all-gather.7
  96.1 87.5 all-gather.5
  185.9 51.0 all-gather.3
where the time goes:
time: 264 us; the launch traced here: 260 us
  waiting for transfers between devices  164 us (62%)
  blocking collectives  60.3 us (23%)
  local copies, waits for them, and re-layouts  14.7 us (6%)
  between operations  13.3 us (5%)
  matrix products  5.86 us (2%)
    all_gather x1, waiting for transfers between devices, on_device(): lax.all_gather(store_down, 'grp', axis=1, tiled=True)  88.4 us
    all_gather x1, waiting for transfers between devices, on_device(): lax.all_gather(store_up, 'grp', axis=1, tiled=True)  73.8 us
    psum x1, blocking collectives, on_device(): shrunk = lax.psum(partial_rank, 'tp')  60.3 us
  transfers between devices with their start and end apart: 3, of which 2 were waited for; matrix products, arithmetic and copies ran while one was open for 7% of the time, Pallas kernels for 0%

commit v1 on v0

v1 whole, which is shorter than its diff:
```python
import functools

import jax
import jax.numpy as jnp
from jax import lax
from jax.experimental import pallas as pl
from jax.experimental.pallas import tpu as pltpu
from jax.sharding import PartitionSpec as P

PIECES = 2
VPG = 4
SLOTS = PIECES * VPG
MESH = pl.DeviceIdType.MESH
F32 = jnp.float32
BF16 = jnp.bfloat16


class Ring:
    def __init__(self, buf, pieces, peers, send, recv):
        self.buf, self.pieces, self.peers = buf, pieces, peers
        self.send, self.recv = send, recv
        self.n = buf.shape[0]
        self.half = self.n // 2
        self.size = buf.shape[1] // pieces

    def events(self):
        for hop in range(1, self.half):
            for index in range(self.pieces):
                yield hop, index
        yield self.half, 0

    def cut(self, way, hop, index):
        if hop == self.half:
            size = self.buf.shape[1] // 2
            return pl.ds(way * size, size)
        piece = index if way == 0 else self.pieces - 1 - index
        return pl.ds(piece * self.size, self.size)

    def slot(self, way, hop):
        return hop % self.n if way == 0 else (self.n - hop) % self.n

    def copy(self, way, hop, index):
        cut = self.cut(way, hop, index)
        return pltpu.make_async_remote_copy(
            src_ref=self.buf.at[self.slot(way, hop - 1), cut],
            dst_ref=self.buf.at[self.slot(way, hop), cut],
            send_sem=self.send.at[way, hop - 1, index],
            recv_sem=self.recv.at[way, hop - 1, index],
            device_id=self.peers[way],
            device_id_type=MESH,
        )

    def start(self):
        for index in range(self.pieces):
            for way in range(2):
                self.copy(way, 1, index).start()

    def advance(self, hop, index):
        for way in range(2):
            self.copy(way, hop, index).wait_recv()
            if hop + 1 < self.half or (hop + 1 == self.half and index == 0):
                self.copy(way, hop + 1, index).start()

    def finish(self):
        for hop, index in self.events():
            for way in range(2):
                self.copy(way, hop, index).wait_send()


def kernel(
    nx, ny, nz,
    act, weight, down, up, home, served, var, out,
    abuf, wbuf, ybuf, ubuf, sel, xsend, xrelay, xrecv, usend, urecv, uother,
    acc, sums, sums_in, whole, parts, parts_in, shrunk, swap, swap_in, table, homes, lists, var_row, var_wide,
    chooser, opener,
    local_sem, z_send, z_recv, y_send, y_recv, u_send, u_recv, x_send, x_recv, v_send, v_recv,
    pair_send, pair_recv, a_send, a_recv, b_send, b_recv,
):
    grp, tp = lax.axis_index("grp"), lax.axis_index("tp")
    x, y = grp // ny, lax.rem(grp, ny)
    z, core = tp // 2, lax.rem(tp, 2)
    tokens = out.shape[0]
    cols = out.shape[1]
    groups = nx * ny
    far = 1 - 2 * core

    def at_x(step):
        return (lax.rem(x + step + nx, nx) * ny + y, tp)

    def at_y(step):
        return (x * ny + lax.rem(y + step + ny, ny), tp)

    def at_z(step):
        return (grp, lax.rem(z + step + nz, nz) * 2 + core)

    other = (grp, z * 2 + 1 - core)

    local = [
        pltpu.make_async_copy(home, homes, local_sem.at[4]),
        pltpu.make_async_copy(served, lists, local_sem.at[5]),
        pltpu.make_async_copy(down, ybuf.at[0], local_sem.at[1]),
        pltpu.make_async_copy(act, abuf.at[0], local_sem.at[0]),
        pltpu.make_async_copy(up, ubuf.at[0], local_sem.at[2]),
        pltpu.make_async_copy(var, var_row, local_sem.at[6]),
        pltpu.make_async_copy(weight.at[:, core], wbuf.at[:, :, pl.ds(0, cols)], local_sem.at[3]),
    ]
    for copy in local:
        copy.start()

    barrier = pltpu.get_barrier_semaphore()
    partners = [other, at_y(1), at_y(-1)] + [at_x(e) for e in range(1, nx)] + [at_z(e) for e in range(1, nz)]
    for partner in partners:
        pl.semaphore_signal(barrier, inc=1, device_id=partner, device_id_type=MESH)

    local[0].wait()
    local[1].wait()

    def fill(k, carry):
        owner = lax.rem(x + k // SLOTS, nx) * ny + y
        j = lax.rem(k, SLOTS)
        table[k] = homes[lists[j // PIECES, owner] * PIECES + lax.rem(j, PIECES)]
        return carry

    lax.fori_loop(0, nx * SLOTS, fill, 0)
    up_rows = up.shape[0] * up.shape[1]
    rank = xrecv.shape[3]

    def set_up():
        shape = chooser.shape
        line = lax.broadcasted_iota(jnp.int32, shape, 0)

        def pick(k, rows):
            return jnp.where((line >> 2) == k, table[k], rows)

        rows = lax.fori_loop(0, nx * SLOTS, pick, jnp.zeros(shape, jnp.int32), unroll=4)
        wanted = rows * 4 + (line & 3)
        chooser[...] = (wanted == lax.broadcasted_iota(jnp.int32, shape, 1)).astype(F32).astype(BF16)
        row = lax.broadcasted_iota(jnp.int32, opener.shape, 0)
        column = lax.broadcasted_iota(jnp.int32, opener.shape, 1)
        hit = (row == ((column >> 4) << 2) + (column & 3)) & (((column >> 2) & 1) == core)
        opener[...] = hit.astype(F32).astype(BF16)
        local[5].wait()
        for i in range(0, tokens, cols):
            size = min(cols, tokens - i)
            row = jnp.broadcast_to(var_row[:, pl.ds(i, size)], (cols, size))
            var_wide[pl.ds(i, size), :] = row.T

    pl.semaphore_wait(barrier, len(partners))

    zring = Ring(abuf, 2, (at_z(1), at_z(-1)), z_send, z_recv)
    yring = Ring(ybuf, 2, (at_y(1), at_y(-1)), y_send, y_recv)
    uring = Ring(ubuf, 1, (at_y(1), at_y(-1)), u_send, u_recv)

    def pair(index, src, dst):
        return pltpu.make_async_remote_copy(
            src_ref=src, dst_ref=dst, send_sem=pair_send.at[index], recv_sem=pair_recv.at[index],
            device_id=other, device_id_type=MESH,
        )

    local[2].wait()
    yring.start()
    local[3].wait()
    zring.start()
    weights = pair(0, weight.at[:, 1 - core], wbuf.at[:, :, pl.ds(cols, cols)])
    weights.start()

    def behind(d):
        return lax.rem(y - d + ny, ny)

    def hand(kind, d):
        mine = x * ny + behind(d)
        passed = lax.rem(x - far + nx, nx) * ny + behind(d)
        straight = d == ny // 2
        src, dst, peer = (
            (xsend.at[d, pl.ds(SLOTS, SLOTS)], xrecv.at[:, mine], at_x(1)),
            (xsend.at[d, pl.ds(3 * SLOTS, SLOTS)], xrecv.at[:, mine], at_x(-1)),
            (
                xsend.at[d, pl.ds(2 * SLOTS, SLOTS)],
                xrecv.at[:, mine] if straight else xrelay.at[d],
                at_x(2) if straight else at_x(far),
            ),
            (xrelay.at[d], xrecv.at[:, passed], at_x(far)),
        )[kind]
        return pltpu.make_async_remote_copy(
            src_ref=src, dst_ref=dst, send_sem=x_send.at[kind, d], recv_sem=x_recv.at[kind, d],
            device_id=peer, device_id_type=MESH,
        )

    def choose(d):
        sel[...] = ybuf[d]
        for e, kind in ((2, 2), (1, 0), (3, 1), (0, None)):

            def take(j, carry):
                xsend[d, e * SLOTS + j] = sel[table[e * SLOTS + j]]
                return carry

            lax.fori_loop(0, SLOTS, take, 0, unroll=True)
            if kind is not None:
                hand(kind, d).start()
        xrecv[:, x * ny + behind(d)] = xsend[d, pl.ds(0, SLOTS)]

    def relay(d):
        if d != ny // 2:
            hand(2, d).wait_recv()
            hand(3, d).start()

    def hand_up(e):
        return pltpu.make_async_remote_copy(
            src_ref=usend.at[e], dst_ref=urecv.at[:, x], send_sem=v_send.at[e - 1], recv_sem=v_recv.at[e - 1],
            device_id=at_x(e), device_id_type=MESH,
        )

    def choose_up(d):
        chosen = jnp.dot(chooser[...], ubuf[d].reshape(up_rows, cols), preferred_element_type=F32)
        chosen = chosen.astype(BF16).reshape(nx, 2, 16, cols)
        for e in range(nx):
            usend[e, :, behind(d)] = chosen[e]

    def multiply(slot, cut):
        home_z = lax.rem(z - slot + nz, nz)
        acc[cut, :] += jnp.dot(abuf[slot, cut, :], wbuf[home_z], preferred_element_type=F32)

    def z_step(event):
        zring.advance(*event)
        hop, index = event
        for way in range(2):
            multiply(zring.slot(way, hop), zring.cut(way, hop, index))

    z_events, y_events, u_events = (list(ring.events()) for ring in (zring, yring, uring))
    choose(0)
    set_up()

    def u_step(event):
        uring.advance(*event)
        for d in sorted({uring.slot(0, event[0]), uring.slot(1, event[0])}):
            choose_up(d)

    waiting = [0]
    last_y = len(y_events) - 1
    for number, (hop, index) in enumerate(y_events):
        yring.advance(hop, index)
        if number == max(last_y - 2, 0):
            local[4].wait()
            uring.start()
        if hop == yring.half or index == 1:
            ready = sorted({yring.slot(0, hop), yring.slot(1, hop)})
            for d in ready:
                choose(d)
            for d in waiting:
                relay(d)
            waiting = ready
        if number == 1:
            local[6].wait()
            weights.wait_recv()
            acc[...] = jnp.dot(abuf[0], wbuf[z], preferred_element_type=F32)
        if number % 2 == 1 and number // 2 < len(z_events) - 4:
            z_step(z_events[number // 2])
    for event in z_events[min(len(y_events) // 2, len(z_events) - 4):-3]:
        z_step(event)
    choose_up(0)
    u_step(u_events[0])

    for d in range(ny):
        for kind in (0, 1, 2 if d == ny // 2 else 3):
            hand(kind, d).wait_recv()
    depth = act.shape[1]
    mine = abuf[0]
    total = jnp.zeros((tokens, PIECES * rank), F32)
    who = jnp.concatenate([var_wide[:, pl.ds(0, rank)]] * PIECES, axis=1)
    for v in range(VPG):
        factor = jnp.concatenate([xrecv[v * PIECES + p].reshape(depth, rank) for p in range(PIECES)], axis=1)
        total = jnp.where(who == v, jnp.dot(mine, factor, preferred_element_type=F32), total)
    for p in range(PIECES):
        sums[p] = total[:, p * rank:(p + 1) * rank]
    first = pair(1, sums.at[1 - core], sums_in)
    first.start()
    if len(u_events) > 2:
        u_step(u_events[1])
    first.wait_recv()
    total = sums[core] + sums_in[...]
    whole[...] = total.reshape(nz, tokens // nz, rank)
    parts[...] = total.astype(BF16).reshape(nz, tokens // nz, rank)

    def scatter(e):
        return pltpu.make_async_remote_copy(
            src_ref=parts.at[lax.rem(z + e, nz)], dst_ref=parts_in.at[e - 1],
            send_sem=a_send.at[e - 1], recv_sem=a_recv.at[e - 1], device_id=at_z(e), device_id_type=MESH,
        )

    def spread(e):
        return pltpu.make_async_remote_copy(
            src_ref=shrunk.at[z], dst_ref=shrunk.at[z],
            send_sem=b_send.at[e - 1], recv_sem=b_recv.at[e - 1], device_id=at_z(e), device_id_type=MESH,
        )

    for e in range(1, nz):
        scatter(e).start()
    z_step(z_events[-3])
    for event in u_events[2 if len(u_events) > 2 else 1:]:
        u_step(event)
    for e in range(1, nx):
        hand_up(e).start()
    urecv[:, x] = usend[0]
    total = whole[z]
    for e in range(1, nz):
        scatter(e).wait_recv()
        total += parts_in[e - 1].astype(F32)
    shrunk[z] = total.astype(BF16)
    for e in range(1, nz):
        spread(e).start()

    for e in range(1, nx):
        hand_up(e).wait_recv()
    ups = pair(2, urecv, uother)
    ups.start()
    for event in z_events[-2:]:
        z_step(event)
    ups.wait_recv()

    wide = groups * 16
    for e in range(1, nz):
        spread(e).wait_recv()
    opened = jnp.dot(shrunk[...].reshape(tokens, rank), opener[...], preferred_element_type=F32)
    total = acc[...]
    who = jnp.concatenate([var_wide[:, pl.ds(0, min(cols, wide))]] * max(wide // cols, 1), axis=1)
    which = (lax.broadcasted_iota(jnp.int32, (1, wide), 1) >> 3) & 1
    for h in range(2):
        part = jnp.where(who == which + 2 * h, opened, 0.0).astype(BF16)
        factor = jnp.concatenate([urecv[h].reshape(wide, cols), uother[h].reshape(wide, cols)], axis=1)
        total += jnp.dot(part, factor, preferred_element_type=F32)
    mine, theirs = total[:, :cols], total[:, cols:]
    swap[...] = theirs
    last = pair(3, swap, swap_in)
    last.start()
    last.wait_recv()
    out[...] = (mine + swap_in[...]).astype(BF16)

    for ring in (zring, yring, uring):
        ring.finish()
    for e in range(1, nx):
        hand_up(e).wait_send()
    for d in range(ny):
        for kind in range(3 if d == ny // 2 else 4):
            hand(kind, d).wait_send()
    for e in range(1, nz):
        scatter(e).wait_send()
        spread(e).wait_send()
    for copy in (weights, first, ups, last):
        copy.wait_send()


def on_device(nx, ny, nz, act, weight, down, up, home, served, var):
    tokens, depth = act.shape
    cols = weight.shape[1]
    blocks, rank = down.shape[0], down.shape[2]
    groups = nx * ny
    served, var = served.T, var.T
    up = up.reshape(blocks * 4 // 16, 16, cols)
    weight = weight.reshape(nz, 2, depth, cols)
    hbm = pl.BlockSpec(memory_space=pl.ANY)
    vmem = pl.BlockSpec(memory_space=pltpu.VMEM)
    dma = pltpu.SemaphoreType.DMA
    share = tokens // nz
    scratch = [
        pltpu.VMEM((nz, tokens, depth), BF16),
        pltpu.VMEM((nz, depth, 2 * cols), BF16),
        pltpu.VMEM((ny,) + down.shape, BF16),
        pltpu.VMEM((ny,) + up.shape, BF16),
        pltpu.VMEM(down.shape, BF16),
        pltpu.VMEM((ny, nx * SLOTS, 16, rank), BF16),
        pltpu.VMEM((ny, SLOTS, 16, rank), BF16),
        pltpu.VMEM((SLOTS, groups, 16, rank), BF16),
        pltpu.VMEM((nx, 2, ny, 16, cols), BF16),
        pltpu.VMEM((2, nx, ny, 16, cols), BF16),
        pltpu.VMEM((2, nx, ny, 16, cols), BF16),
        pltpu.VMEM((tokens, 2 * cols), F32),
        pltpu.VMEM((2, tokens, rank), F32),
        pltpu.VMEM((tokens, rank), F32),
        pltpu.VMEM((nz, share, rank), F32),
        pltpu.VMEM((nz, share, rank), BF16),
        pltpu.VMEM((nz - 1, share, rank), BF16),
        pltpu.VMEM((nz, share, rank), BF16),
        pltpu.VMEM((tokens, cols), F32),
        pltpu.VMEM((tokens, cols), F32),
        pltpu.SMEM((nx * SLOTS,), jnp.int32),
        pltpu.SMEM(home.shape, jnp.int32),
        pltpu.SMEM(served.shape, jnp.int32),
        pltpu.VMEM(var.shape, jnp.int32),
        pltpu.VMEM((tokens, cols), jnp.int32),
        pltpu.VMEM((nx * SLOTS * 4, blocks * 4), BF16),
        pltpu.VMEM((rank, groups * 16), BF16),
        dma((7,)),
        dma((2, nz // 2, 2)), dma((2, nz // 2, 2)),
        dma((2, ny // 2, 2)), dma((2, ny // 2, 2)),
        dma((2, ny // 2, 1)), dma((2, ny // 2, 1)),
        dma((4, ny)), dma((4, ny)),
        dma((nx - 1,)), dma((nx - 1,)),
        dma((4,)), dma((4,)),
        dma((nz - 1,)), dma((nz - 1,)),
        dma((nz - 1,)), dma((nz - 1,)),
    ]
    return pl.pallas_call(
        functools.partial(kernel, nx, ny, nz),
        out_shape=jax.ShapeDtypeStruct((tokens, cols), BF16),
        in_specs=[hbm] * 7,
        out_specs=vmem,
        scratch_shapes=scratch,
        compiler_params=pltpu.CompilerParams(
            collective_id=0, has_side_effects=True, vmem_limit_bytes=56 * 1024 * 1024
        ),
    )(act, weight, down, up, home, served, var)


def solution(mesh):
    nx = 4
    ny, nz = mesh.shape["grp"] // nx, mesh.shape["tp"] // 2
    in_specs = (
        P("grp", "tp"),
        P(None, "tp"),
        P(None, ("tp", "grp"), None),
        P(None, "grp", "tp"),
        P(),
        P(),
        P("grp", None),
    )
    return jax.shard_map(
        functools.partial(on_device, nx, ny, nz),
        mesh=mesh, in_specs=in_specs, out_specs=P("grp", "tp"), check_vma=False,
    )
```

time: 264 us -> 53 us (0.20); the launches traced: 260 us -> 52.8 us
  waiting for transfers between devices: 164 us -> 0 us
  blocking collectives: 60.3 us -> 0 us
  Pallas kernels: 0 us -> 51.3 us
  between operations: 13.3 us -> 0.01 us
  local copies, waits for them, and re-layouts: 14.7 us -> 1.47 us
  matrix products: 5.86 us -> 0 us
    all_gather x3 -> x0, waiting for transfers between devices: 162 us -> none  [the longest x1 88.4 us: on_device(): lax.all_gather(store_down, 'grp', axis=1, tiled=True)]
    psum x1 -> x0, blocking collectives: 60.3 us -> none  [on_device(): shrunk = lax.psum(partial_rank, 'tp')]
    pallas_call x0 -> x1, Pallas kernels: none -> 51.3 us  [on_device(): pl.pallas_call(functools.partial(kernel, nx, ny, nz), out_shape=jax.Shape...]
    gather x5 -> x0, local copies, waits for them, and re-layouts: 9.47 us -> none  [the longest x1 3.34 us: on_device(): activations[source_row]]
    dot_general x3 -> x0, matrix products: 5.86 us -> none  [the longest x1 4.06 us: on_device(): jnp.dot(lax.all_gather(activations, 'tp', axis=1, tiled=True), kv_weight,...]
  transfers between devices with their start and end apart: 3 -> 0, of which waited for: 2 -> 0; matrix products, arithmetic and copies ran while one was open for 7% -> 0% of each run, Pallas kernels for 0% -> 0%
where the time goes in v1:
time: 53 us; the launch traced here: 52.8 us
  Pallas kernels  51.3 us (97%)
  local copies, waits for them, and re-layouts  1.47 us (3%)
    pallas_call x1, Pallas kernels, on_device(): pl.pallas_call(functools.partial(kernel, nx, ny, nz), out_shape=jax.Shape...  51.3 us
    unnamed x1, local copies, waits for them, and re-layouts  1.47 us

profile of v1, /device:TPU:1, one launch (start us, length us, event | category | flops | bytes accessed | tf_op | source)
XLA Modules:
  0.0 52.8 jit_solution(12409122073626346200)
XLA Ops:
  0.0 51.3 %shard_map.73 = bf16[256,128]{1,0:T(8,128)(2,1)} custom-call(bf16[256,512]{1,0:T(8,128)(2,1)} %act.1, bf16[8,2,512,128]{3,2,1,0:T(8,128)(2,1)} %bitcast.4, bf16[32,16,128]{2,1,0:T(8,128)(2,1)} %down.1, bf16[8,16,128]{2,1,0:T(8,128)(2,1)} %bitcast.5, s32[32]{0:T(128)} %home.1, s32[4,32]{1,0:T(4,128)} %bitcast.6, s32[1,256]{1,0:T(1,128)} %bitcast.7), custom_call_target="tpu_custom_call" | custom-call | tf_op jit(solution)/shard_map/pallas_call | solution.py:402
  51.4 1.5 %copy.9 = bf16[256,128]{1,0:T(8,128)(2,1)} copy(bf16[256,128]{1,0:T(8,128)(2,1)} %shard_map.73) | data formatting | bytes 131072

commit v2 on v1

--- a/solution.py
+++ b/solution.py
@@ -70,8 +70,8 @@
 def kernel(
     nx, ny, nz,
     act, weight, down, up, home, served, var, out,
-    abuf, wbuf, ybuf, ubuf, sel, xsend, xrelay, xrecv, usend, urecv, uother,
-    acc, sums, sums_in, whole, parts, parts_in, shrunk, swap, swap_in, table, homes, lists, var_row, var_wide,
+    abuf, wmine, wother, ybuf, ubuf, sel, xsend, xrelay, xrecv, usend, urecv,
+    acc, sums, sums_in, whole, parts, parts_in, shrunk, swap_in, table, homes, lists, var_row, var_wide,
     chooser, opener,
     local_sem, z_send, z_recv, y_send, y_recv, u_send, u_recv, x_send, x_recv, v_send, v_recv,
     pair_send, pair_recv, a_send, a_recv, b_send, b_recv,
@@ -90,8 +90,8 @@
     def at_y(step):
         return (x * ny + lax.rem(y + step + ny, ny), tp)
 
-    def at_z(step):
-        return (grp, lax.rem(z + step + nz, nz) * 2 + core)
+    def at_z(step, side=0):
+        return (grp, lax.rem(z + step + nz, nz) * 2 + (core if side == 0 else 1 - core))
 
     other = (grp, z * 2 + 1 - core)
 
@@ -102,13 +102,14 @@
         pltpu.make_async_copy(act, abuf.at[0], local_sem.at[0]),
         pltpu.make_async_copy(up, ubuf.at[0], local_sem.at[2]),
         pltpu.make_async_copy(var, var_row, local_sem.at[6]),
-        pltpu.make_async_copy(weight.at[:, core], wbuf.at[:, :, pl.ds(0, cols)], local_sem.at[3]),
+        pltpu.make_async_copy(weight.at[:, core], wmine, local_sem.at[3]),
     ]
     for copy in local:
         copy.start()
 
     barrier = pltpu.get_barrier_semaphore()
-    partners = [other, at_y(1), at_y(-1)] + [at_x(e) for e in range(1, nx)] + [at_z(e) for e in range(1, nz)]
+    partners = [other] + [at_y(e) for e in range(1, ny)] + [at_x(e) for e in range(1, nx)]
+    partners += [at_z(e, side) for side in range(2) for e in range(1, nz)]
     for partner in partners:
         pl.semaphore_signal(barrier, inc=1, device_id=partner, device_id_type=MESH)
 
@@ -123,7 +124,9 @@
 
     lax.fori_loop(0, nx * SLOTS, fill, 0)
     up_rows = up.shape[0] * up.shape[1]
-    rank = xrecv.shape[3]
+    rank = xrecv.shape[-1]
+    depth = act.shape[1]
+    share = tokens // nz
 
     def set_up():
         shape = chooser.shape
@@ -137,7 +140,8 @@
         chooser[...] = (wanted == lax.broadcasted_iota(jnp.int32, shape, 1)).astype(F32).astype(BF16)
         row = lax.broadcasted_iota(jnp.int32, opener.shape, 0)
         column = lax.broadcasted_iota(jnp.int32, opener.shape, 1)
-        hit = (row == ((column >> 4) << 2) + (column & 3)) & (((column >> 2) & 1) == core)
+        piece = (column >> 2) & 1
+        hit = row == piece * rank + ((column >> 4) << 2) + (column & 3)
         opener[...] = hit.astype(F32).astype(BF16)
         local[5].wait()
         for i in range(0, tokens, cols):
@@ -149,7 +153,6 @@
 
     zring = Ring(abuf, 2, (at_z(1), at_z(-1)), z_send, z_recv)
     yring = Ring(ybuf, 2, (at_y(1), at_y(-1)), y_send, y_recv)
-    uring = Ring(ubuf, 1, (at_y(1), at_y(-1)), u_send, u_recv)
 
     def pair(index, src, dst):
         return pltpu.make_async_remote_copy(
@@ -161,7 +164,7 @@
     yring.start()
     local[3].wait()
     zring.start()
-    weights = pair(0, weight.at[:, 1 - core], wbuf.at[:, :, pl.ds(cols, cols)])
+    weights = pair(0, weight.at[:, 1 - core], wother)
     weights.start()
 
     def behind(d):
@@ -172,14 +175,14 @@
         passed = lax.rem(x - far + nx, nx) * ny + behind(d)
         straight = d == ny // 2
         src, dst, peer = (
-            (xsend.at[d, pl.ds(SLOTS, SLOTS)], xrecv.at[:, mine], at_x(1)),
-            (xsend.at[d, pl.ds(3 * SLOTS, SLOTS)], xrecv.at[:, mine], at_x(-1)),
+            (xsend.at[d, pl.ds(SLOTS, SLOTS)], xrecv.at[mine], at_x(1)),
+            (xsend.at[d, pl.ds(3 * SLOTS, SLOTS)], xrecv.at[mine], at_x(-1)),
             (
                 xsend.at[d, pl.ds(2 * SLOTS, SLOTS)],
-                xrecv.at[:, mine] if straight else xrelay.at[d],
+                xrecv.at[mine] if straight else xrelay.at[d],
                 at_x(2) if straight else at_x(far),
             ),
-            (xrelay.at[d], xrecv.at[:, passed], at_x(far)),
+            (xrelay.at[d], xrecv.at[passed], at_x(far)),
         )[kind]
         return pltpu.make_async_remote_copy(
             src_ref=src, dst_ref=dst, send_sem=x_send.at[kind, d], recv_sem=x_recv.at[kind, d],
@@ -197,51 +200,57 @@
             lax.fori_loop(0, SLOTS, take, 0, unroll=True)
             if kind is not None:
                 hand(kind, d).start()
-        xrecv[:, x * ny + behind(d)] = xsend[d, pl.ds(0, SLOTS)]
+        xrecv[x * ny + behind(d)] = xsend[d, pl.ds(0, SLOTS)]
 
     def relay(d):
         if d != ny // 2:
             hand(2, d).wait_recv()
             hand(3, d).start()
 
+    def spread_up(e):
+        return pltpu.make_async_remote_copy(
+            src_ref=ubuf.at[0], dst_ref=ubuf.at[e], send_sem=u_send.at[e - 1], recv_sem=u_recv.at[e - 1],
+            device_id=at_y(e), device_id_type=MESH,
+        )
+
     def hand_up(e):
         return pltpu.make_async_remote_copy(
-            src_ref=usend.at[e], dst_ref=urecv.at[:, x], send_sem=v_send.at[e - 1], recv_sem=v_recv.at[e - 1],
+            src_ref=usend.at[e], dst_ref=urecv.at[x], send_sem=v_send.at[e - 1], recv_sem=v_recv.at[e - 1],
             device_id=at_x(e), device_id_type=MESH,
         )
 
-    def choose_up(d):
-        chosen = jnp.dot(chooser[...], ubuf[d].reshape(up_rows, cols), preferred_element_type=F32)
-        chosen = chosen.astype(BF16).reshape(nx, 2, 16, cols)
-        for e in range(nx):
-            usend[e, :, behind(d)] = chosen[e]
+    def choose_up():
+        blocks = jnp.concatenate([ubuf[d].reshape(up_rows, cols) for d in range(ny)], axis=1)
+        chosen = jnp.dot(chooser[...], blocks, preferred_element_type=F32).astype(BF16)
+        for d in range(ny):
+            some = chosen[:, d * cols:(d + 1) * cols].reshape(nx, 2, 16, cols)
+            for e in range(nx):
+                usend[e, :, behind(d)] = some[e]
 
     def multiply(slot, cut):
-        home_z = lax.rem(z - slot + nz, nz)
-        acc[cut, :] += jnp.dot(abuf[slot, cut, :], wbuf[home_z], preferred_element_type=F32)
-
-    def z_step(event):
-        zring.advance(*event)
+        place = lax.rem(z - slot + nz, nz)
+        both = jnp.concatenate([wmine[place], wother[place]], axis=1)
+        return jnp.dot(abuf[slot, cut, :], both, preferred_element_type=F32)
+
+    def z_multiply(event):
         hop, index = event
         for way in range(2):
-            multiply(zring.slot(way, hop), zring.cut(way, hop, index))
-
-    z_events, y_events, u_events = (list(ring.events()) for ring in (zring, yring, uring))
+            cut = zring.cut(way, hop, index)
+            acc[cut, :] += multiply(zring.slot(way, hop), cut)
+
+    z_events, y_events = (list(ring.events()) for ring in (zring, yring))
     choose(0)
     set_up()
 
-    def u_step(event):
-        uring.advance(*event)
-        for d in sorted({uring.slot(0, event[0]), uring.slot(1, event[0])}):
-            choose_up(d)
-
     waiting = [0]
     last_y = len(y_events) - 1
+    early = min(len(y_events) // 2, len(z_events) - 4)
     for number, (hop, index) in enumerate(y_events):
         yring.advance(hop, index)
         if number == max(last_y - 2, 0):
             local[4].wait()
-            uring.start()
+            for e in range(1, ny):
+                spread_up(e).start()
         if hop == yring.half or index == 1:
             ready = sorted({yring.slot(0, hop), yring.slot(1, hop)})
             for d in ready:
@@ -249,37 +258,35 @@
             for d in waiting:
                 relay(d)
             waiting = ready
-        if number == 1:
-            local[6].wait()
-            weights.wait_recv()
-            acc[...] = jnp.dot(abuf[0], wbuf[z], preferred_element_type=F32)
-        if number % 2 == 1 and number // 2 < len(z_events) - 4:
-            z_step(z_events[number // 2])
-    for event in z_events[min(len(y_events) // 2, len(z_events) - 4):-3]:
-        z_step(event)
-    choose_up(0)
-    u_step(u_events[0])
+        if number % 2 == 1 and number // 2 < early:
+            zring.advance(*z_events[number // 2])
+    for event in z_events[early:-3]:
+        zring.advance(*event)
+    local[6].wait()
+    weights.wait_recv()
+    acc[...] = multiply(0, pl.ds(0, tokens))
+    z_multiply(z_events[0])
 
     for d in range(ny):
         for kind in (0, 1, 2 if d == ny // 2 else 3):
             hand(kind, d).wait_recv()
-    depth = act.shape[1]
     mine = abuf[0]
     total = jnp.zeros((tokens, PIECES * rank), F32)
     who = jnp.concatenate([var_wide[:, pl.ds(0, rank)]] * PIECES, axis=1)
     for v in range(VPG):
-        factor = jnp.concatenate([xrecv[v * PIECES + p].reshape(depth, rank) for p in range(PIECES)], axis=1)
+        factor = jnp.concatenate([xrecv[:, v * PIECES + p].reshape(depth, rank) for p in range(PIECES)], axis=1)
         total = jnp.where(who == v, jnp.dot(mine, factor, preferred_element_type=F32), total)
     for p in range(PIECES):
         sums[p] = total[:, p * rank:(p + 1) * rank]
     first = pair(1, sums.at[1 - core], sums_in)
     first.start()
-    if len(u_events) > 2:
-        u_step(u_events[1])
+    zring.advance(*z_events[-3])
+    for event in z_events[1:-4]:
+        z_multiply(event)
     first.wait_recv()
     total = sums[core] + sums_in[...]
-    whole[...] = total.reshape(nz, tokens // nz, rank)
-    parts[...] = total.astype(BF16).reshape(nz, tokens // nz, rank)
+    whole[...] = total.reshape(nz, share, rank)
+    parts[...] = total.astype(BF16).reshape(nz, share, rank)
 
     def scatter(e):
         return pltpu.make_async_remote_copy(
@@ -287,55 +294,58 @@
             send_sem=a_send.at[e - 1], recv_sem=a_recv.at[e - 1], device_id=at_z(e), device_id_type=MESH,
         )
 
-    def spread(e):
-        return pltpu.make_async_remote_copy(
-            src_ref=shrunk.at[z], dst_ref=shrunk.at[z],
-            send_sem=b_send.at[e - 1], recv_sem=b_recv.at[e - 1], device_id=at_z(e), device_id_type=MESH,
-        )
+    def spread(e, side):
+        return pltpu.make_async_remote_copy(
+            src_ref=shrunk.at[core, z], dst_ref=shrunk.at[core, z],
+            send_sem=b_send.at[side, e], recv_sem=b_recv.at[side, e],
+            device_id=at_z(e, side), device_id_type=MESH,
+        )
+
+    targets = [(e, side) for e in range(1, nz) for side in range(2)] + [(0, 1)]
 
     for e in range(1, nz):
         scatter(e).start()
-    z_step(z_events[-3])
-    for event in u_events[2 if len(u_events) > 2 else 1:]:
-        u_step(event)
+    for e in range(1, ny):
+        spread_up(e).wait_recv()
+    choose_up()
     for e in range(1, nx):
         hand_up(e).start()
-    urecv[:, x] = usend[0]
+    urecv[x] = usend[0]
     total = whole[z]
     for e in range(1, nz):
         scatter(e).wait_recv()
         total += parts_in[e - 1].astype(F32)
-    shrunk[z] = total.astype(BF16)
-    for e in range(1, nz):
-        spread(e).start()
-
+    shrunk[core, z] = total.astype(BF16)
+    for target in targets:
+        spread(*target).start()
+
+    zring.advance(*z_events[-2])
+    for event in z_events[-4:-1]:
+        z_multiply(event)
+    zring.advance(*z_events[-1])
+    z_multiply(z_events[-1])
+    last = pair(2, acc.at[:, pl.ds(cols, cols)], swap_in)
+    last.start()
+
+    wide = groups * 16
     for e in range(1, nx):
         hand_up(e).wait_recv()
-    ups = pair(2, urecv, uother)
-    ups.start()
-    for event in z_events[-2:]:
-        z_step(event)
-    ups.wait_recv()
-
-    wide = groups * 16
-    for e in range(1, nz):
-        spread(e).wait_recv()
-    opened = jnp.dot(shrunk[...].reshape(tokens, rank), opener[...], preferred_element_type=F32)
-    total = acc[...]
+    for target in targets:
+        spread(*target).wait_recv()
+    both = jnp.concatenate([shrunk[p].reshape(tokens, rank) for p in range(PIECES)], axis=1)
+    opened = jnp.dot(both, opener[...], preferred_element_type=F32)
+    total = acc[:, pl.ds(0, cols)]
     who = jnp.concatenate([var_wide[:, pl.ds(0, min(cols, wide))]] * max(wide // cols, 1), axis=1)
     which = (lax.broadcasted_iota(jnp.int32, (1, wide), 1) >> 3) & 1
     for h in range(2):
         part = jnp.where(who == which + 2 * h, opened, 0.0).astype(BF16)
-        factor = jnp.concatenate([urecv[h].reshape(wide, cols), uother[h].reshape(wide, cols)], axis=1)
-        total += jnp.dot(part, factor, preferred_element_type=F32)
-    mine, theirs = total[:, :cols], total[:, cols:]
-    swap[...] = theirs
-    last = pair(3, swap, swap_in)
-    last.start()
+        total += jnp.dot(part, urecv[:, h].reshape(wide, cols), preferred_element_type=F32)
     last.wait_recv()
-    out[...] = (mine + swap_in[...]).astype(BF16)
-
-    for ring in (zring, yring, uring):
+    out[...] = (total + swap_in[...]).astype(BF16)
+
+    for e in range(1, ny):
+        spread_up(e).wait_send()
+    for ring in (zring, yring):
         ring.finish()
     for e in range(1, nx):
         hand_up(e).wait_send()
@@ -344,8 +354,9 @@
             hand(kind, d).wait_send()
     for e in range(1, nz):
         scatter(e).wait_send()
-        spread(e).wait_send()
-    for copy in (weights, first, ups, last):
+    for target in targets:
+        spread(*target).wait_send()
+    for copy in (weights, first, last):
         copy.wait_send()
 
 
@@ -363,24 +374,23 @@
     share = tokens // nz
     scratch = [
         pltpu.VMEM((nz, tokens, depth), BF16),
-        pltpu.VMEM((nz, depth, 2 * cols), BF16),
+        pltpu.VMEM((nz, depth, cols), BF16),
+        pltpu.VMEM((nz, depth, cols), BF16),
         pltpu.VMEM((ny,) + down.shape, BF16),
         pltpu.VMEM((ny,) + up.shape, BF16),
         pltpu.VMEM(down.shape, BF16),
         pltpu.VMEM((ny, nx * SLOTS, 16, rank), BF16),
         pltpu.VMEM((ny, SLOTS, 16, rank), BF16),
-        pltpu.VMEM((SLOTS, groups, 16, rank), BF16),
+        pltpu.VMEM((groups, SLOTS, 16, rank), BF16),
         pltpu.VMEM((nx, 2, ny, 16, cols), BF16),
-        pltpu.VMEM((2, nx, ny, 16, cols), BF16),
-        pltpu.VMEM((2, nx, ny, 16, cols), BF16),
+        pltpu.VMEM((nx, 2, ny, 16, cols), BF16),
         pltpu.VMEM((tokens, 2 * cols), F32),
         pltpu.VMEM((2, tokens, rank), F32),
         pltpu.VMEM((tokens, rank), F32),
         pltpu.VMEM((nz, share, rank), F32),
         pltpu.VMEM((nz, share, rank), BF16),
         pltpu.VMEM((nz - 1, share, rank), BF16),
-        pltpu.VMEM((nz, share, rank), BF16),
-        pltpu.VMEM((tokens, cols), F32),
+        pltpu.VMEM((PIECES, nz, share, rank), BF16),
         pltpu.VMEM((tokens, cols), F32),
         pltpu.SMEM((nx * SLOTS,), jnp.int32),
         pltpu.SMEM(home.shape, jnp.int32),
@@ -388,16 +398,16 @@
         pltpu.VMEM(var.shape, jnp.int32),
         pltpu.VMEM((tokens, cols), jnp.int32),
         pltpu.VMEM((nx * SLOTS * 4, blocks * 4), BF16),
-        pltpu.VMEM((rank, groups * 16), BF16),
+        pltpu.VMEM((PIECES * rank, groups * 16), BF16),
         dma((7,)),
         dma((2, nz // 2, 2)), dma((2, nz // 2, 2)),
         dma((2, ny // 2, 2)), dma((2, ny // 2, 2)),
-        dma((2, ny // 2, 1)), dma((2, ny // 2, 1)),
+        dma((ny - 1,)), dma((ny - 1,)),
         dma((4, ny)), dma((4, ny)),
         dma((nx - 1,)), dma((nx - 1,)),
-        dma((4,)), dma((4,)),
+        dma((3,)), dma((3,)),
         dma((nz - 1,)), dma((nz - 1,)),
-        dma((nz - 1,)), dma((nz - 1,)),
+        dma((2, nz)), dma((2, nz)),
     ]
     return pl.pallas_call(
         functools.partial(kernel, nx, ny, nz),

time: 53 us -> 54.2 us (1.023)
  Pallas kernels: 51.3 us -> 52.2 us
    pallas_call x1, Pallas kernels: 51.3 us -> 52.2 us  [on_device(): pl.pallas_call(functools.partial(kernel, nx, ny, nz), out_shape=jax.Shape...]
where the time goes in v2:
time: 54.2 us; the launch traced here: 53.7 us
  Pallas kernels  52.2 us (96%)
  local copies, waits for them, and re-layouts  1.47 us (3%)
    pallas_call x1, Pallas kernels, on_device(): pl.pallas_call(functools.partial(kernel, nx, ny, nz), out_shape=jax.Shape...  52.2 us
    unnamed x1, local copies, waits for them, and re-layouts  1.47 us

profile of v2, /device:TPU:1, one launch (start us, length us, event | category | flops | bytes accessed | tf_op | source)
XLA Modules:
  0.0 53.7 jit_solution(1959442316896572740)
XLA Ops:
  0.0 52.2 %shard_map.73 = bf16[256,128]{1,0:T(8,128)(2,1)} custom-call(bf16[256,512]{1,0:T(8,128)(2,1)} %act.1, bf16[8,2,512,128]{3,2,1,0:T(8,128)(2,1)} %bitcast.4, bf16[32,16,128]{2,1,0:T(8,128)(2,1)} %down.1, bf16[8,16,128]{2,1,0:T(8,128)(2,1)} %bitcast.5, s32[32]{0:T(128)} %home.1, s32[4,32]{1,0:T(4,128)} %bitcast.6, s32[1,256]{1,0:T(1,128)} %bitcast.7), custom_call_target="tpu_custom_call" | custom-call | tf_op jit(solution)/shard_map/pallas_call | solution.py:412
  52.2 1.5 %copy.9 = bf16[256,128]{1,0:T(8,128)(2,1)} copy(bf16[256,128]{1,0:T(8,128)(2,1)} %shard_map.73) | data formatting | bytes 131072

commit v3 on v2

v3 whole, which is shorter than its diff:
```python
import functools

import jax
import jax.numpy as jnp
from jax import lax
from jax.experimental import pallas as pl
from jax.experimental.pallas import tpu as pltpu
from jax.sharding import PartitionSpec as P

PIECES = 2
VPG = 4
SLOTS = PIECES * VPG
MESH = pl.DeviceIdType.MESH
F32 = jnp.float32
BF16 = jnp.bfloat16


class Ring:
    def __init__(self, buf, pieces, peers, send, recv):
        self.buf, self.pieces, self.peers = buf, pieces, peers
        self.send, self.recv = send, recv
        self.n = buf.shape[0]
        self.half = self.n // 2
        self.size = buf.shape[1] // pieces

    def events(self):
        for hop in range(1, self.half):
            for index in range(self.pieces):
                yield hop, index
        yield self.half, 0

    def cut(self, way, hop, index):
        if hop == self.half:
            size = self.buf.shape[1] // 2
            return pl.ds(way * size, size)
        piece = index if way == 0 else self.pieces - 1 - index
        return pl.ds(piece * self.size, self.size)

    def slot(self, way, hop):
        return hop % self.n if way == 0 else (self.n - hop) % self.n

    def copy(self, way, hop, index):
        cut = self.cut(way, hop, index)
        return pltpu.make_async_remote_copy(
            src_ref=self.buf.at[self.slot(way, hop - 1), cut],
            dst_ref=self.buf.at[self.slot(way, hop), cut],
            send_sem=self.send,
            recv_sem=self.recv.at[way, hop - 1, index],
            device_id=self.peers[way],
            device_id_type=MESH,
        )

    def start(self):
        for index in range(self.pieces):
            for way in range(2):
                self.copy(way, 1, index).start()

    def advance(self, hop, index):
        for way in range(2):
            self.copy(way, hop, index).wait_recv()
            if hop + 1 < self.half or (hop + 1 == self.half and index == 0):
                self.copy(way, hop + 1, index).start()


def loop(first, end, body):
    def step(k, carry):
        body(k)
        return carry

    lax.fori_loop(first, end, step, 0)


def kernel(
    nx, ny, nz,
    act, weight, down, up, home, served, var, out,
    abuf, wmine, wother, ybuf, ubuf, sel, xsend, xrelay, xrecv, usend, urecv,
    acc, sums, sums_in, whole, parts, parts_in, shrunk, swap_in, table, homes, lists, var_row, var_wide,
    chooser, opener,
    permuted, local_sem, z_recv, y_recv, relay_recv, sent, got, pair_send, pair_recv,
):
    grp, tp = lax.axis_index("grp"), lax.axis_index("tp")
    x, y = grp // ny, lax.rem(grp, ny)
    z, core = tp // 2, lax.rem(tp, 2)
    tokens = out.shape[0]
    cols = out.shape[1]
    groups = nx * ny
    far = 1 - 2 * core

    def at_x(step):
        return (lax.rem(x + step + nx, nx) * ny + y, tp)

    def at_y(step):
        return (x * ny + lax.rem(y + step + ny, ny), tp)

    def at_z(step, side=0):
        return (grp, lax.rem(z + step + nz, nz) * 2 + (core if side == 0 else 1 - core))

    other = (grp, z * 2 + 1 - core)

    local = [
        pltpu.make_async_copy(home, homes, local_sem.at[4]),
        pltpu.make_async_copy(served, lists, local_sem.at[5]),
        pltpu.make_async_copy(down, ybuf.at[0], local_sem.at[1]),
        pltpu.make_async_copy(act, abuf.at[0], local_sem.at[0]),
        pltpu.make_async_copy(up, ubuf.at[0], local_sem.at[2]),
        pltpu.make_async_copy(var, var_row, local_sem.at[6]),
        pltpu.make_async_copy(weight.at[:, core], wmine, local_sem.at[3]),
    ]
    for copy in local:
        copy.start()

    barrier = pltpu.get_barrier_semaphore()

    def greet(partner):
        pl.semaphore_signal(barrier, inc=1, device_id=partner, device_id_type=MESH)

    greet(other)
    loop(1, ny, lambda e: greet(at_y(e)))
    loop(1, nx, lambda e: greet(at_x(e)))
    loop(1, nz, lambda e: [greet(at_z(e, side)) for side in range(2)])

    local[0].wait()
    local[1].wait()

    def fill(k, carry):
        owner = lax.rem(x + k // SLOTS, nx) * ny + y
        j = lax.rem(k, SLOTS)
        table[k] = homes[lists[j // PIECES, owner] * PIECES + lax.rem(j, PIECES)]
        return carry

    lax.fori_loop(0, nx * SLOTS, fill, 0)
    up_rows = up.shape[0] * up.shape[1]
    rank = xrecv.shape[-1]
    depth = act.shape[1]
    share = tokens // nz

    def set_up():
        shape = chooser.shape
        line = lax.broadcasted_iota(jnp.int32, shape, 0)

        def pick(k, rows):
            return jnp.where((line >> 2) == k, table[k], rows)

        rows = lax.fori_loop(0, nx * SLOTS, pick, jnp.zeros(shape, jnp.int32), unroll=4)
        wanted = rows * 4 + (line & 3)
        chooser[...] = (wanted == lax.broadcasted_iota(jnp.int32, shape, 1)).astype(F32).astype(BF16)
        row = lax.broadcasted_iota(jnp.int32, opener.shape, 0)
        column = lax.broadcasted_iota(jnp.int32, opener.shape, 1)
        piece = (column >> 2) & 1
        hit = row == piece * rank + ((column >> 4) << 2) + (column & 3)
        opener[...] = hit.astype(F32).astype(BF16)
        for e in range(nx):
            width = ny * 16
            row = lax.broadcasted_iota(jnp.int32, (depth, width), 0)
            column = lax.broadcasted_iota(jnp.int32, (depth, width), 1)
            place = column >> 4
            behind_y = jnp.where((place & 1) == 1, (place + 1) >> 1, ny - (place >> 1))
            from_group = lax.rem(x + nx - e, nx) * ny + ((y - behind_y) & (ny - 1))
            hit = (row >> 4 == from_group) & ((row & 15) == (column & 15))
            columns = jnp.dot(abuf[0], hit.astype(F32).astype(BF16), preferred_element_type=F32)
            permuted[:, e * width:(e + 1) * width] = columns.astype(BF16)
        local[5].wait()
        for i in range(0, tokens, cols):
            size = min(cols, tokens - i)
            row = jnp.broadcast_to(var_row[:, pl.ds(i, size)], (cols, size))
            var_wide[pl.ds(i, size), :] = row.T

    pl.semaphore_wait(barrier, ny + nx + 2 * nz - 3)

    zring = Ring(abuf, 2, (at_z(1), at_z(-1)), sent.at[0], z_recv)
    yring = Ring(ybuf, 2, (at_y(1), at_y(-1)), sent.at[1], y_recv)

    def pair(index, src, dst):
        return pltpu.make_async_remote_copy(
            src_ref=src, dst_ref=dst, send_sem=pair_send.at[index], recv_sem=pair_recv.at[index],
            device_id=other, device_id_type=MESH,
        )

    local[2].wait()
    yring.start()
    local[3].wait()
    zring.start()
    weights = pair(0, weight.at[:, 1 - core], wother)
    weights.start()

    def behind(d):
        return lax.rem(y - d + ny, ny)

    def remote(src, dst, send, recv, peer):
        return pltpu.make_async_remote_copy(
            src_ref=src, dst_ref=dst, send_sem=send, recv_sem=recv, device_id=peer, device_id_type=MESH
        )

    def all_sent(kind, ref):
        remote(ref, ref, sent.at[kind], got.at[0], other).wait_send()

    def all_got(kind, ref):
        remote(ref, ref, sent.at[0], got.at[kind], other).wait_recv()

    groups_of_places = [(0, 1)] + [(2 * k - 1, 2) for k in range(1, ny // 2)] + [(ny - 1, 1)]

    def chunk(place):
        return (place + 1) // 2 if place % 2 else (ny - place // 2) % ny

    def hand(e, number):
        places = pl.ds(*groups_of_places[number])
        if e == 2 and number != len(groups_of_places) - 1:
            return remote(xsend.at[2, places], xrelay.at[places], sent.at[2], relay_recv.at[number], at_x(far))
        return remote(xsend.at[e, places], xrecv.at[e, places], sent.at[2], got.at[1], at_x(e))

    def choose(number):
        first, count = groups_of_places[number]
        for place in range(first, first + count):
            sel[place - first] = ybuf[chunk(place)]
        for e in (2, 1, 3, 0):

            def take(j):
                slot = table[e * SLOTS + j]
                for k in range(count):
                    if e == 0:
                        xrecv[0, first + k, j] = sel[k, slot]
                    else:
                        xsend[e, first + k, j] = sel[k, slot]

            loop(0, SLOTS, take)
            if e:
                hand(e, number).start()

    def relay(number):
        if number != len(groups_of_places) - 1:
            hand(2, number).wait_recv()
            places = pl.ds(*groups_of_places[number])
            remote(xrelay.at[places], xrecv.at[2, places], sent.at[3], got.at[1], at_x(far)).start()

    def spread_up(e):
        return remote(ubuf.at[0], ubuf.at[e], sent.at[4], got.at[2], at_y(e))

    def hand_up(e):
        return remote(usend.at[e], urecv.at[x], sent.at[5], got.at[3], at_x(e))

    def choose_up():
        blocks = jnp.concatenate([ubuf[d].reshape(up_rows, cols) for d in range(ny)], axis=1)
        chosen = jnp.dot(chooser[...], blocks, preferred_element_type=F32).astype(BF16)
        for d in range(ny):
            some = chosen[:, d * cols:(d + 1) * cols].reshape(nx, 2, 16, cols)
            for e in range(nx):
                usend[e, :, behind(d)] = some[e]

    def multiply(slot):
        place = lax.rem(z - slot + nz, nz)
        both = jnp.concatenate([wmine[place], wother[place]], axis=1)
        return jnp.dot(abuf[slot], both, preferred_element_type=F32)

    def multiply_pair(hop):
        def add(k):
            acc[...] += multiply(hop + k * (nz - 2 * hop))

        loop(0, 2, add)

    z_events, y_events = (list(ring.events()) for ring in (zring, yring))
    choose(0)
    set_up()

    last_y = len(y_events) - 1
    for number, (hop, index) in enumerate(y_events):
        yring.advance(hop, index)
        if number == max(last_y - 2, 0):
            local[4].wait()
            loop(1, ny, lambda e: spread_up(e).start())
        if hop == yring.half or index == 1:
            choose(hop)
            relay(hop - 1)
        if number % 2 == 1 and number // 2 < len(z_events) - 4:
            zring.advance(*z_events[number // 2])
    for event in z_events[min(len(y_events) // 2, len(z_events) - 4):-3]:
        zring.advance(*event)
    local[6].wait()
    weights.wait_recv()
    acc[...] = multiply(0)
    multiply_pair(1)

    all_got(1, xrecv.at[pl.ds(1, nx - 1)])
    mine = permuted[...]
    total = jnp.zeros((tokens, PIECES * rank), F32)
    who = jnp.concatenate([var_wide[:, pl.ds(0, rank)]] * PIECES, axis=1)
    for v in range(VPG):
        factor = jnp.concatenate([xrecv[:, :, v * PIECES + p].reshape(depth, rank) for p in range(PIECES)], axis=1)
        total = jnp.where(who == v, jnp.dot(mine, factor, preferred_element_type=F32), total)
    for p in range(PIECES):
        sums[p] = total[:, p * rank:(p + 1) * rank]
    first = pair(1, sums.at[1 - core], sums_in)
    first.start()
    zring.advance(*z_events[-3])
    for hop in range(2, nz // 2 - 1):
        multiply_pair(hop)
    first.wait_recv()
    total = sums[core] + sums_in[...]
    whole[...] = total.reshape(nz, share, rank)
    parts[...] = total.astype(BF16).reshape(nz, share, rank)

    def scatter(e):
        return remote(parts.at[lax.rem(z + e, nz)], parts_in.at[e - 1], sent.at[6], got.at[4], at_z(e))

    def spread(e, side):
        shard = shrunk.at[core * nz + z]
        return remote(shard, shard, sent.at[7], got.at[5], at_z(e, side))

    loop(1, nz, lambda e: scatter(e).start())
    all_got(2, ubuf.at[pl.ds(1, ny - 1)])
    choose_up()
    loop(1, nx, lambda e: hand_up(e).start())
    urecv[x] = usend[0]
    all_got(4, parts_in)
    shrunk[core * nz + z] = (whole[z] + jnp.sum(parts_in[...].astype(F32), axis=0)).astype(BF16)
    loop(1, nz, lambda e: [spread(e, side).start() for side in range(2)])
    spread(0, 1).start()

    zring.advance(*z_events[-2])
    multiply_pair(nz // 2 - 1)
    zring.advance(*z_events[-1])
    acc[...] += multiply(nz // 2)
    last = pair(2, acc.at[:, pl.ds(cols, cols)], swap_in)
    last.start()

    all_sent(0, abuf.at[pl.ds(0, nz - 1)])
    all_sent(1, ybuf.at[pl.ds(0, ny - 1)])
    all_sent(2, xsend.at[pl.ds(1, nx - 1)])
    all_sent(3, xrelay)
    all_sent(4, ubuf.at[pl.ds(0, ny - 1)])
    all_sent(5, usend.at[pl.ds(1, nx - 1)])
    all_sent(6, parts.at[pl.ds(0, nz - 1)])
    weights.wait_send()
    first.wait_send()
    all_got(3, urecv.at[pl.ds(0, nx - 1)])
    all_got(5, shrunk.at[pl.ds(0, 2 * nz - 1)])
    wide = groups * 16
    both = jnp.concatenate([shrunk[pl.ds(p * nz, nz)].reshape(tokens, rank) for p in range(PIECES)], axis=1)
    opened = jnp.dot(both, opener[...], preferred_element_type=F32)
    total = acc[:, pl.ds(0, cols)]
    who = jnp.concatenate([var_wide[:, pl.ds(0, min(cols, wide))]] * max(wide // cols, 1), axis=1)
    which = (lax.broadcasted_iota(jnp.int32, (1, wide), 1) >> 3) & 1
    for h in range(2):
        part = jnp.where(who == which + 2 * h, opened, 0.0).astype(BF16)
        total += jnp.dot(part, urecv[:, h].reshape(wide, cols), preferred_element_type=F32)
    last.wait_recv()
    out[...] = (total + swap_in[...]).astype(BF16)

    all_sent(7, shrunk.at[pl.ds(0, 2 * nz - 1)])
    last.wait_send()


def on_device(nx, ny, nz, act, weight, down, up, home, served, var):
    tokens, depth = act.shape
    cols = weight.shape[1]
    blocks, rank = down.shape[0], down.shape[2]
    groups = nx * ny
    served, var = served.T, var.T
    up = up.reshape(blocks * 4 // 16, 16, cols)
    weight = weight.reshape(nz, 2, depth, cols)
    hbm = pl.BlockSpec(memory_space=pl.ANY)
    vmem = pl.BlockSpec(memory_space=pltpu.VMEM)
    dma = pltpu.SemaphoreType.DMA
    share = tokens // nz
    scratch = [
        pltpu.VMEM((nz, tokens, depth), BF16),
        pltpu.VMEM((nz, depth, cols), BF16),
        pltpu.VMEM((nz, depth, cols), BF16),
        pltpu.VMEM((ny,) + down.shape, BF16),
        pltpu.VMEM((ny,) + up.shape, BF16),
        pltpu.VMEM((2,) + down.shape, BF16),
        pltpu.VMEM((nx, ny, SLOTS, 16, rank), BF16),
        pltpu.VMEM((ny - 1, SLOTS, 16, rank), BF16),
        pltpu.VMEM((nx, ny, SLOTS, 16, rank), BF16),
        pltpu.VMEM((nx, 2, ny, 16, cols), BF16),
        pltpu.VMEM((nx, 2, ny, 16, cols), BF16),
        pltpu.VMEM((tokens, 2 * cols), F32),
        pltpu.VMEM((2, tokens, rank), F32),
        pltpu.VMEM((tokens, rank), F32),
        pltpu.VMEM((nz, share, rank), F32),
        pltpu.VMEM((nz, share, rank), BF16),
        pltpu.VMEM((nz - 1, share, rank), BF16),
        pltpu.VMEM((PIECES * nz, share, rank), BF16),
        pltpu.VMEM((tokens, cols), F32),
        pltpu.SMEM((nx * SLOTS,), jnp.int32),
        pltpu.SMEM(home.shape, jnp.int32),
        pltpu.SMEM(served.shape, jnp.int32),
        pltpu.VMEM(var.shape, jnp.int32),
        pltpu.VMEM((tokens, cols), jnp.int32),
        pltpu.VMEM((nx * SLOTS * 4, blocks * 4), BF16),
        pltpu.VMEM((PIECES * rank, groups * 16), BF16),
        pltpu.VMEM((tokens, depth), BF16),
        dma((7,)),
        dma((2, nz // 2, 2)), dma((2, ny // 2, 2)), dma((ny // 2,)),
        dma((8,)), dma((6,)), dma((3,)), dma((3,)),
    ]
    return pl.pallas_call(
        functools.partial(kernel, nx, ny, nz),
        out_shape=jax.ShapeDtypeStruct((tokens, cols), BF16),
        in_specs=[hbm] * 7,
        out_specs=vmem,
        scratch_shapes=scratch,
        compiler_params=pltpu.CompilerParams(
            collective_id=0, has_side_effects=True, vmem_limit_bytes=56 * 1024 * 1024
        ),
    )(act, weight, down, up, home, served, var)


def solution(mesh):
    nx = 4
    ny, nz = mesh.shape["grp"] // nx, mesh.shape["tp"] // 2
    in_specs = (
        P("grp", "tp"),
        P(None, "tp"),
        P(None, ("tp", "grp"), None),
        P(None, "grp", "tp"),
        P(),
        P(),
        P("grp", None),
    )
    return jax.shard_map(
        functools.partial(on_device, nx, ny, nz),
        mesh=mesh, in_specs=in_specs, out_specs=P("grp", "tp"), check_vma=False,
    )
```

time: 54.2 us -> 52.8 us (0.974)
  Pallas kernels: 52.2 us -> 50.6 us
    pallas_call x1, Pallas kernels: 52.2 us -> 50.6 us  [on_device(): pl.pallas_call(functools.partial(kernel, nx, ny, nz), out_shape=jax.Shape...]
where the time goes in v3:
time: 52.8 us; the launch traced here: 52.1 us
  Pallas kernels  50.6 us (96%)
  local copies, waits for them, and re-layouts  1.47 us (3%)
    pallas_call x1, Pallas kernels, on_device(): pl.pallas_call(functools.partial(kernel, nx, ny, nz), out_shape=jax.Shape...  50.6 us
    unnamed x1, local copies, waits for them, and re-layouts  1.47 us

profile of v3, /device:TPU:1, one launch (start us, length us, event | category | flops | bytes accessed | tf_op | source)
XLA Modules:
  0.0 52.1 jit_solution(4956509785189824326)
XLA Ops:
  0.0 50.6 %shard_map.73 = bf16[256,128]{1,0:T(8,128)(2,1)} custom-call(bf16[256,512]{1,0:T(8,128)(2,1)} %act.1, bf16[8,2,512,128]{3,2,1,0:T(8,128)(2,1)} %bitcast.4, bf16[32,16,128]{2,1,0:T(8,128)(2,1)} %down.1, bf16[8,16,128]{2,1,0:T(8,128)(2,1)} %bitcast.5, s32[32]{0:T(128)} %home.1, s32[4,32]{1,0:T(4,128)} %bitcast.6, s32[1,256]{1,0:T(1,128)} %bitcast.7), custom_call_target="tpu_custom_call" | custom-call | tf_op jit(solution)/shard_map/pallas_call | solution.py:396
  50.6 1.5 %copy.9 = bf16[256,128]{1,0:T(8,128)(2,1)} copy(bf16[256,128]{1,0:T(8,128)(2,1)} %shard_map.73) | data formatting | bytes 131072

commit v4 on v3

--- a/solution.py
+++ b/solution.py
@@ -73,7 +73,7 @@
 def kernel(
     nx, ny, nz,
     act, weight, down, up, home, served, var, out,
-    abuf, wmine, wother, ybuf, ubuf, sel, xsend, xrelay, xrecv, usend, urecv,
+    abuf, wmine, wother, ybuf, sel, xsend, xrelay, xrecv,
     acc, sums, sums_in, whole, parts, parts_in, shrunk, swap_in, table, homes, lists, var_row, var_wide,
     chooser, opener,
     permuted, local_sem, z_recv, y_recv, relay_recv, sent, got, pair_send, pair_recv,
@@ -84,6 +84,7 @@
     tokens = out.shape[0]
     cols = out.shape[1]
     groups = nx * ny
+    blocks = down.shape[0]
     far = 1 - 2 * core
 
     def at_x(step):
@@ -100,9 +101,9 @@
     local = [
         pltpu.make_async_copy(home, homes, local_sem.at[4]),
         pltpu.make_async_copy(served, lists, local_sem.at[5]),
-        pltpu.make_async_copy(down, ybuf.at[0], local_sem.at[1]),
+        pltpu.make_async_copy(down, ybuf.at[0, pl.ds(0, blocks)], local_sem.at[1]),
         pltpu.make_async_copy(act, abuf.at[0], local_sem.at[0]),
-        pltpu.make_async_copy(up, ubuf.at[0], local_sem.at[2]),
+        pltpu.make_async_copy(up, ybuf.at[0, pl.ds(blocks, up.shape[0])], local_sem.at[2]),
         pltpu.make_async_copy(var, var_row, local_sem.at[6]),
         pltpu.make_async_copy(weight.at[:, core], wmine, local_sem.at[3]),
     ]
@@ -115,7 +116,8 @@
         pl.semaphore_signal(barrier, inc=1, device_id=partner, device_id_type=MESH)
 
     greet(other)
-    loop(1, ny, lambda e: greet(at_y(e)))
+    greet(at_y(1))
+    greet(at_y(-1))
     loop(1, nx, lambda e: greet(at_x(e)))
     loop(1, nz, lambda e: [greet(at_z(e, side)) for side in range(2)])
 
@@ -134,7 +136,7 @@
     depth = act.shape[1]
     share = tokens // nz
 
-    def set_up():
+    def set_up_choice():
         shape = chooser.shape
         line = lax.broadcasted_iota(jnp.int32, shape, 0)
 
@@ -144,28 +146,30 @@
         rows = lax.fori_loop(0, nx * SLOTS, pick, jnp.zeros(shape, jnp.int32), unroll=4)
         wanted = rows * 4 + (line & 3)
         chooser[...] = (wanted == lax.broadcasted_iota(jnp.int32, shape, 1)).astype(F32).astype(BF16)
-        row = lax.broadcasted_iota(jnp.int32, opener.shape, 0)
-        column = lax.broadcasted_iota(jnp.int32, opener.shape, 1)
-        piece = (column >> 2) & 1
-        hit = row == piece * rank + ((column >> 4) << 2) + (column & 3)
-        opener[...] = hit.astype(F32).astype(BF16)
+
+    def set_up():
+        width = ny * 16
+        place = lax.broadcasted_iota(jnp.int32, (1, width), 1) >> 4
+        behind_y = jnp.where((place & 1) == 1, (place + 1) >> 1, ny - (place >> 1))
         for e in range(nx):
-            width = ny * 16
+            columns = pl.ds(e * width, width)
+            from_group = lax.rem(x + nx - e, nx) * ny + ((y - behind_y) & (ny - 1))
             row = lax.broadcasted_iota(jnp.int32, (depth, width), 0)
             column = lax.broadcasted_iota(jnp.int32, (depth, width), 1)
-            place = column >> 4
-            behind_y = jnp.where((place & 1) == 1, (place + 1) >> 1, ny - (place >> 1))
-            from_group = lax.rem(x + nx - e, nx) * ny + ((y - behind_y) & (ny - 1))
-            hit = (row >> 4 == from_group) & ((row & 15) == (column & 15))
-            columns = jnp.dot(abuf[0], hit.astype(F32).astype(BF16), preferred_element_type=F32)
-            permuted[:, e * width:(e + 1) * width] = columns.astype(BF16)
+            hit = row == from_group * 16 + (column & 15)
+            moved = jnp.dot(abuf[0], hit.astype(F32).astype(BF16), preferred_element_type=F32)
+            permuted[:, columns] = moved.astype(BF16)
+            row = lax.broadcasted_iota(jnp.int32, (PIECES * rank, width), 0)
+            column = lax.broadcasted_iota(jnp.int32, (PIECES * rank, width), 1)
+            hit = row == ((column >> 2) & 1) * rank + from_group * 4 + (column & 3)
+            opener[:, columns] = hit.astype(F32).astype(BF16)
         local[5].wait()
         for i in range(0, tokens, cols):
             size = min(cols, tokens - i)
             row = jnp.broadcast_to(var_row[:, pl.ds(i, size)], (cols, size))
             var_wide[pl.ds(i, size), :] = row.T
 
-    pl.semaphore_wait(barrier, ny + nx + 2 * nz - 3)
+    pl.semaphore_wait(barrier, nx + 2 * nz)
 
     zring = Ring(abuf, 2, (at_z(1), at_z(-1)), sent.at[0], z_recv)
     yring = Ring(ybuf, 2, (at_y(1), at_y(-1)), sent.at[1], y_recv)
@@ -177,11 +181,11 @@
         )
 
     local[2].wait()
+    local[4].wait()
     yring.start()
     local[3].wait()
     zring.start()
     weights = pair(0, weight.at[:, 1 - core], wother)
-    weights.start()
 
     def behind(d):
         return lax.rem(y - d + ny, ny)
@@ -210,8 +214,11 @@
 
     def choose(number):
         first, count = groups_of_places[number]
-        for place in range(first, first + count):
-            sel[place - first] = ybuf[chunk(place)]
+        chunks = [chunk(first + k) for k in range(count)]
+        ups = [ybuf[d, pl.ds(blocks, up.shape[0])].reshape(up_rows, cols) for d in chunks]
+        chosen = jnp.dot(chooser[...], jnp.concatenate(ups, axis=1), preferred_element_type=F32).astype(BF16)
+        for k in range(count):
+            sel[k] = ybuf[chunks[k], pl.ds(0, blocks)]
         for e in (2, 1, 3, 0):
 
             def take(j):
@@ -223,6 +230,12 @@
                         xsend[e, first + k, j] = sel[k, slot]
 
             loop(0, SLOTS, take)
+            for k in range(count):
+                rows = chosen[e * SLOTS * 4:(e + 1) * SLOTS * 4, k * cols:(k + 1) * cols].reshape(2, 16, cols)
+                if e == 0:
+                    xrecv[0, first + k, pl.ds(SLOTS, 2)] = rows
+                else:
+                    xsend[e, first + k, pl.ds(SLOTS, 2)] = rows
             if e:
                 hand(e, number).start()
 
@@ -232,20 +245,6 @@
             places = pl.ds(*groups_of_places[number])
             remote(xrelay.at[places], xrecv.at[2, places], sent.at[3], got.at[1], at_x(far)).start()
 
-    def spread_up(e):
-        return remote(ubuf.at[0], ubuf.at[e], sent.at[4], got.at[2], at_y(e))
-
-    def hand_up(e):
-        return remote(usend.at[e], urecv.at[x], sent.at[5], got.at[3], at_x(e))
-
-    def choose_up():
-        blocks = jnp.concatenate([ubuf[d].reshape(up_rows, cols) for d in range(ny)], axis=1)
-        chosen = jnp.dot(chooser[...], blocks, preferred_element_type=F32).astype(BF16)
-        for d in range(ny):
-            some = chosen[:, d * cols:(d + 1) * cols].reshape(nx, 2, 16, cols)
-            for e in range(nx):
-                usend[e, :, behind(d)] = some[e]
-
     def multiply(slot):
         place = lax.rem(z - slot + nz, nz)
         both = jnp.concatenate([wmine[place], wother[place]], axis=1)
@@ -258,15 +257,15 @@
         loop(0, 2, add)
 
     z_events, y_events = (list(ring.events()) for ring in (zring, yring))
+    set_up_choice()
     choose(0)
     set_up()
 
     last_y = len(y_events) - 1
     for number, (hop, index) in enumerate(y_events):
         yring.advance(hop, index)
-        if number == max(last_y - 2, 0):
-            local[4].wait()
-            loop(1, ny, lambda e: spread_up(e).start())
+        if number == min(1, last_y):
+            weights.start()
         if hop == yring.half or index == 1:
             choose(hop)
             relay(hop - 1)
@@ -299,18 +298,14 @@
     parts[...] = total.astype(BF16).reshape(nz, share, rank)
 
     def scatter(e):
-        return remote(parts.at[lax.rem(z + e, nz)], parts_in.at[e - 1], sent.at[6], got.at[4], at_z(e))
+        return remote(parts.at[lax.rem(z + e, nz)], parts_in.at[e - 1], sent.at[4], got.at[2], at_z(e))
 
     def spread(e, side):
         shard = shrunk.at[core * nz + z]
-        return remote(shard, shard, sent.at[7], got.at[5], at_z(e, side))
+        return remote(shard, shard, sent.at[5], got.at[3], at_z(e, side))
 
     loop(1, nz, lambda e: scatter(e).start())
-    all_got(2, ubuf.at[pl.ds(1, ny - 1)])
-    choose_up()
-    loop(1, nx, lambda e: hand_up(e).start())
-    urecv[x] = usend[0]
-    all_got(4, parts_in)
+    all_got(2, parts_in)
     shrunk[core * nz + z] = (whole[z] + jnp.sum(parts_in[...].astype(F32), axis=0)).astype(BF16)
     loop(1, nz, lambda e: [spread(e, side).start() for side in range(2)])
     spread(0, 1).start()
@@ -326,13 +321,10 @@
     all_sent(1, ybuf.at[pl.ds(0, ny - 1)])
     all_sent(2, xsend.at[pl.ds(1, nx - 1)])
     all_sent(3, xrelay)
-    all_sent(4, ubuf.at[pl.ds(0, ny - 1)])
-    all_sent(5, usend.at[pl.ds(1, nx - 1)])
-    all_sent(6, parts.at[pl.ds(0, nz - 1)])
+    all_sent(4, parts.at[pl.ds(0, nz - 1)])
     weights.wait_send()
     first.wait_send()
-    all_got(3, urecv.at[pl.ds(0, nx - 1)])
-    all_got(5, shrunk.at[pl.ds(0, 2 * nz - 1)])
+    all_got(3, shrunk.at[pl.ds(0, 2 * nz - 1)])
     wide = groups * 16
     both = jnp.concatenate([shrunk[pl.ds(p * nz, nz)].reshape(tokens, rank) for p in range(PIECES)], axis=1)
     opened = jnp.dot(both, opener[...], preferred_element_type=F32)
@@ -341,11 +333,11 @@
     which = (lax.broadcasted_iota(jnp.int32, (1, wide), 1) >> 3) & 1
     for h in range(2):
         part = jnp.where(who == which + 2 * h, opened, 0.0).astype(BF16)
-        total += jnp.dot(part, urecv[:, h].reshape(wide, cols), preferred_element_type=F32)
+        total += jnp.dot(part, xrecv[:, :, SLOTS + h].reshape(wide, cols), preferred_element_type=F32)
     last.wait_recv()
     out[...] = (total + swap_in[...]).astype(BF16)
 
-    all_sent(7, shrunk.at[pl.ds(0, 2 * nz - 1)])
+    all_sent(5, shrunk.at[pl.ds(0, 2 * nz - 1)])
     last.wait_send()
 
 
@@ -365,14 +357,11 @@
         pltpu.VMEM((nz, tokens, depth), BF16),
         pltpu.VMEM((nz, depth, cols), BF16),
         pltpu.VMEM((nz, depth, cols), BF16),
-        pltpu.VMEM((ny,) + down.shape, BF16),
-        pltpu.VMEM((ny,) + up.shape, BF16),
+        pltpu.VMEM((ny, blocks + up.shape[0], 16, rank), BF16),
         pltpu.VMEM((2,) + down.shape, BF16),
-        pltpu.VMEM((nx, ny, SLOTS, 16, rank), BF16),
-        pltpu.VMEM((ny - 1, SLOTS, 16, rank), BF16),
-        pltpu.VMEM((nx, ny, SLOTS, 16, rank), BF16),
-        pltpu.VMEM((nx, 2, ny, 16, cols), BF16),
-        pltpu.VMEM((nx, 2, ny, 16, cols), BF16),
+        pltpu.VMEM((nx, ny, SLOTS + 2, 16, rank), BF16),
+        pltpu.VMEM((ny - 1, SLOTS + 2, 16, rank), BF16),
+        pltpu.VMEM((nx, ny, SLOTS + 2, 16, rank), BF16),
         pltpu.VMEM((tokens, 2 * cols), F32),
         pltpu.VMEM((2, tokens, rank), F32),
         pltpu.VMEM((tokens, rank), F32),
@@ -391,7 +380,7 @@
         pltpu.VMEM((tokens, depth), BF16),
         dma((7,)),
         dma((2, nz // 2, 2)), dma((2, ny // 2, 2)), dma((ny // 2,)),
-        dma((8,)), dma((6,)), dma((3,)), dma((3,)),
+        dma((6,)), dma((4,)), dma((3,)), dma((3,)),
     ]
     return pl.pallas_call(
         functools.partial(kernel, nx, ny, nz),

time: 52.8 us -> 54 us (1.023)
  Pallas kernels: 50.6 us -> 52.3 us
    pallas_call x1, Pallas kernels: 50.6 us -> 52.3 us  [on_device(): pl.pallas_call(functools.partial(kernel, nx, ny, nz), out_shape=jax.Shape...]
where the time goes in v4:
time: 54 us; the launch traced here: 53.8 us
  Pallas kernels  52.3 us (97%)
  local copies, waits for them, and re-layouts  1.47 us (3%)
    pallas_call x1, Pallas kernels, on_device(): pl.pallas_call(functools.partial(kernel, nx, ny, nz), out_shape=jax.Shape...  52.3 us
    unnamed x1, local copies, waits for them, and re-layouts  1.47 us

profile of v4, /device:TPU:1, one launch (start us, length us, event | category | flops | bytes accessed | tf_op | source)
XLA Modules:
  0.0 53.8 jit_solution(8801329763650916591)
XLA Ops:
  0.0 52.3 %shard_map.73 = bf16[256,128]{1,0:T(8,128)(2,1)} custom-call(bf16[256,512]{1,0:T(8,128)(2,1)} %act.1, bf16[8,2,512,128]{3,2,1,0:T(8,128)(2,1)} %bitcast.4, bf16[32,16,128]{2,1,0:T(8,128)(2,1)} %down.1, bf16[8,16,128]{2,1,0:T(8,128)(2,1)} %bitcast.5, s32[32]{0:T(128)} %home.1, s32[4,32]{1,0:T(4,128)} %bitcast.6, s32[1,256]{1,0:T(1,128)} %bitcast.7), custom_call_target="tpu_custom_call" | custom-call | tf_op jit(solution)/shard_map/pallas_call | solution.py:385
  52.3 1.5 %copy.9 = bf16[256,128]{1,0:T(8,128)(2,1)} copy(bf16[256,128]{1,0:T(8,128)(2,1)} %shard_map.73) | data formatting | bytes 131072

commit v5 on v4

--- a/solution.py
+++ b/solution.py
@@ -27,12 +27,10 @@
         for hop in range(1, self.half):
             for index in range(self.pieces):
                 yield hop, index
-        yield self.half, 0
-
-    def cut(self, way, hop, index):
-        if hop == self.half:
-            size = self.buf.shape[1] // 2
-            return pl.ds(way * size, size)
+        for index in range(self.pieces // 2):
+            yield self.half, index
+
+    def cut(self, way, index):
         piece = index if way == 0 else self.pieces - 1 - index
         return pl.ds(piece * self.size, self.size)
 
@@ -40,7 +38,7 @@
         return hop % self.n if way == 0 else (self.n - hop) % self.n
 
     def copy(self, way, hop, index):
-        cut = self.cut(way, hop, index)
+        cut = self.cut(way, index)
         return pltpu.make_async_remote_copy(
             src_ref=self.buf.at[self.slot(way, hop - 1), cut],
             dst_ref=self.buf.at[self.slot(way, hop), cut],
@@ -58,7 +56,7 @@
     def advance(self, hop, index):
         for way in range(2):
             self.copy(way, hop, index).wait_recv()
-            if hop + 1 < self.half or (hop + 1 == self.half and index == 0):
+            if hop + 1 < self.half or (hop + 1 == self.half and index < self.pieces // 2):
                 self.copy(way, hop + 1, index).start()
 
 
@@ -74,7 +72,7 @@
     nx, ny, nz,
     act, weight, down, up, home, served, var, out,
     abuf, wmine, wother, ybuf, sel, xsend, xrelay, xrecv,
-    acc, sums, sums_in, whole, parts, parts_in, shrunk, swap_in, table, homes, lists, var_row, var_wide,
+    acc, whole, parts, parts_in, shrunk, swap_in, table, homes, lists, var_row, var_wide,
     chooser, opener,
     permuted, local_sem, z_recv, y_recv, relay_recv, sent, got, pair_send, pair_recv,
 ):
@@ -147,22 +145,32 @@
         wanted = rows * 4 + (line & 3)
         chooser[...] = (wanted == lax.broadcasted_iota(jnp.int32, shape, 1)).astype(F32).astype(BF16)
 
-    def set_up():
+    def sources(e):
         width = ny * 16
         place = lax.broadcasted_iota(jnp.int32, (1, width), 1) >> 4
         behind_y = jnp.where((place & 1) == 1, (place + 1) >> 1, ny - (place >> 1))
+        return pl.ds(e * width, width), lax.rem(x + nx - e, nx) * ny + ((y - behind_y) & (ny - 1))
+
+    def set_up():
         for e in range(nx):
-            columns = pl.ds(e * width, width)
-            from_group = lax.rem(x + nx - e, nx) * ny + ((y - behind_y) & (ny - 1))
+            columns, from_group = sources(e)
+            width = ny * 16
             row = lax.broadcasted_iota(jnp.int32, (depth, width), 0)
             column = lax.broadcasted_iota(jnp.int32, (depth, width), 1)
             hit = row == from_group * 16 + (column & 15)
             moved = jnp.dot(abuf[0], hit.astype(F32).astype(BF16), preferred_element_type=F32)
             permuted[:, columns] = moved.astype(BF16)
+
+    def set_up_last():
+        for e in range(nx):
+            columns, from_group = sources(e)
+            width = ny * 16
             row = lax.broadcasted_iota(jnp.int32, (PIECES * rank, width), 0)
             column = lax.broadcasted_iota(jnp.int32, (PIECES * rank, width), 1)
             hit = row == ((column >> 2) & 1) * rank + from_group * 4 + (column & 3)
             opener[:, columns] = hit.astype(F32).astype(BF16)
+
+    def set_up_tokens():
         local[5].wait()
         for i in range(0, tokens, cols):
             size = min(cols, tokens - i)
@@ -172,7 +180,7 @@
     pl.semaphore_wait(barrier, nx + 2 * nz)
 
     zring = Ring(abuf, 2, (at_z(1), at_z(-1)), sent.at[0], z_recv)
-    yring = Ring(ybuf, 2, (at_y(1), at_y(-1)), sent.at[1], y_recv)
+    yring = Ring(ybuf, 4, (at_y(1), at_y(-1)), sent.at[1], y_recv)
 
     def pair(index, src, dst):
         return pltpu.make_async_remote_copy(
@@ -229,7 +237,8 @@
                     else:
                         xsend[e, first + k, j] = sel[k, slot]
 
-            loop(0, SLOTS, take)
+            for j in range(SLOTS):
+                take(j)
             for k in range(count):
                 rows = chosen[e * SLOTS * 4:(e + 1) * SLOTS * 4, k * cols:(k + 1) * cols].reshape(2, 16, cols)
                 if e == 0:
@@ -261,22 +270,18 @@
     choose(0)
     set_up()
 
-    last_y = len(y_events) - 1
     for number, (hop, index) in enumerate(y_events):
         yring.advance(hop, index)
-        if number == min(1, last_y):
-            weights.start()
-        if hop == yring.half or index == 1:
+        if number + 1 == len(y_events) or y_events[number + 1][0] > hop:
             choose(hop)
             relay(hop - 1)
-        if number % 2 == 1 and number // 2 < len(z_events) - 4:
-            zring.advance(*z_events[number // 2])
-    for event in z_events[min(len(y_events) // 2, len(z_events) - 4):-3]:
+            if hop == 1:
+                weights.start()
+        if hop > 1 and index == 1:
+            zring.advance(*z_events[hop - 2])
+    set_up_tokens()
+    for event in z_events[yring.half - 1:-3]:
         zring.advance(*event)
-    local[6].wait()
-    weights.wait_recv()
-    acc[...] = multiply(0)
-    multiply_pair(1)
 
     all_got(1, xrecv.at[pl.ds(1, nx - 1)])
     mine = permuted[...]
@@ -286,44 +291,47 @@
         factor = jnp.concatenate([xrecv[:, :, v * PIECES + p].reshape(depth, rank) for p in range(PIECES)], axis=1)
         total = jnp.where(who == v, jnp.dot(mine, factor, preferred_element_type=F32), total)
     for p in range(PIECES):
-        sums[p] = total[:, p * rank:(p + 1) * rank]
-    first = pair(1, sums.at[1 - core], sums_in)
-    first.start()
-    zring.advance(*z_events[-3])
-    for hop in range(2, nz // 2 - 1):
-        multiply_pair(hop)
-    first.wait_recv()
-    total = sums[core] + sums_in[...]
-    whole[...] = total.reshape(nz, share, rank)
-    parts[...] = total.astype(BF16).reshape(nz, share, rank)
-
-    def scatter(e):
-        return remote(parts.at[lax.rem(z + e, nz)], parts_in.at[e - 1], sent.at[4], got.at[2], at_z(e))
+        part = total[:, p * rank:(p + 1) * rank]
+        parts[p] = part.astype(BF16).reshape(nz, share, rank)
+        whole[p] = part.reshape(nz, share, rank)
+
+    def scatter(e, side):
+        source = parts.at[core if side == 0 else 1 - core, lax.rem(z + e, nz)]
+        return remote(source, parts_in.at[side * nz + e], sent.at[4], got.at[2], at_z(e, side))
 
     def spread(e, side):
         shard = shrunk.at[core * nz + z]
         return remote(shard, shard, sent.at[5], got.at[3], at_z(e, side))
 
-    loop(1, nz, lambda e: scatter(e).start())
-    all_got(2, parts_in)
-    shrunk[core * nz + z] = (whole[z] + jnp.sum(parts_in[...].astype(F32), axis=0)).astype(BF16)
+    loop(1, nz, lambda e: [scatter(e, side).start() for side in range(2)])
+    scatter(0, 1).start()
+    zring.advance(*z_events[-3])
+    set_up_last()
+    local[6].wait()
+    weights.wait_recv()
+    acc[...] = multiply(0)
+    multiply_pair(1)
+    all_got(2, parts_in.at[pl.ds(1, 2 * nz - 1)])
+    others = jnp.sum(parts_in[pl.ds(1, 2 * nz - 1)].astype(F32), axis=0)
+    shrunk[core * nz + z] = (whole[core, z] + others).astype(BF16)
     loop(1, nz, lambda e: [spread(e, side).start() for side in range(2)])
     spread(0, 1).start()
+    for hop in range(2, nz // 2 - 1):
+        multiply_pair(hop)
 
     zring.advance(*z_events[-2])
     multiply_pair(nz // 2 - 1)
     zring.advance(*z_events[-1])
     acc[...] += multiply(nz // 2)
-    last = pair(2, acc.at[:, pl.ds(cols, cols)], swap_in)
+    last = pair(1, acc.at[:, pl.ds(cols, cols)], swap_in)
     last.start()
 
     all_sent(0, abuf.at[pl.ds(0, nz - 1)])
     all_sent(1, ybuf.at[pl.ds(0, ny - 1)])
     all_sent(2, xsend.at[pl.ds(1, nx - 1)])
     all_sent(3, xrelay)
-    all_sent(4, parts.at[pl.ds(0, nz - 1)])
+    all_sent(4, parts_in.at[pl.ds(1, 2 * nz - 1)])
     weights.wait_send()
-    first.wait_send()
     all_got(3, shrunk.at[pl.ds(0, 2 * nz - 1)])
     wide = groups * 16
     both = jnp.concatenate([shrunk[pl.ds(p * nz, nz)].reshape(tokens, rank) for p in range(PIECES)], axis=1)
@@ -363,11 +371,9 @@
         pltpu.VMEM((ny - 1, SLOTS + 2, 16, rank), BF16),
         pltpu.VMEM((nx, ny, SLOTS + 2, 16, rank), BF16),
         pltpu.VMEM((tokens, 2 * cols), F32),
-        pltpu.VMEM((2, tokens, rank), F32),
-        pltpu.VMEM((tokens, rank), F32),
-        pltpu.VMEM((nz, share, rank), F32),
-        pltpu.VMEM((nz, share, rank), BF16),
-        pltpu.VMEM((nz - 1, share, rank), BF16),
+        pltpu.VMEM((PIECES, nz, share, rank), F32),
+        pltpu.VMEM((PIECES, nz, share, rank), BF16),
+        pltpu.VMEM((2 * nz, share, rank), BF16),
         pltpu.VMEM((PIECES * nz, share, rank), BF16),
         pltpu.VMEM((tokens, cols), F32),
         pltpu.SMEM((nx * SLOTS,), jnp.int32),
@@ -379,8 +385,8 @@
         pltpu.VMEM((PIECES * rank, groups * 16), BF16),
         pltpu.VMEM((tokens, depth), BF16),
         dma((7,)),
-        dma((2, nz // 2, 2)), dma((2, ny // 2, 2)), dma((ny // 2,)),
-        dma((6,)), dma((4,)), dma((3,)), dma((3,)),
+        dma((2, nz // 2, 2)), dma((2, ny // 2, 4)), dma((ny // 2,)),
+        dma((6,)), dma((4,)), dma((2,)), dma((2,)),
     ]
     return pl.pallas_call(
         functools.partial(kernel, nx, ny, nz),

time: 54 us -> 54.1 us (level)
  no operation moved by 1% of the time
where the time goes in v5:
time: 54.1 us; the launch traced here: 54 us
  Pallas kernels  52.5 us (97%)
  local copies, waits for them, and re-layouts  1.47 us (3%)
    pallas_call x1, Pallas kernels, on_device(): pl.pallas_call(functools.partial(kernel, nx, ny, nz), out_shape=jax.Shape...  52.5 us
    unnamed x1, local copies, waits for them, and re-layouts  1.47 us

profile of v5, /device:TPU:1, one launch (start us, length us, event | category | flops | bytes accessed | tf_op | source)
XLA Modules:
  0.0 54.0 jit_solution(5930325587346551651)
XLA Ops:
  0.0 52.5 %shard_map.73 = bf16[256,128]{1,0:T(8,128)(2,1)} custom-call(bf16[256,512]{1,0:T(8,128)(2,1)} %act.1, bf16[8,2,512,128]{3,2,1,0:T(8,128)(2,1)} %bitcast.4, bf16[32,16,128]{2,1,0:T(8,128)(2,1)} %down.1, bf16[8,16,128]{2,1,0:T(8,128)(2,1)} %bitcast.5, s32[32]{0:T(128)} %home.1, s32[4,32]{1,0:T(4,128)} %bitcast.6, s32[1,256]{1,0:T(1,128)} %bitcast.7), custom_call_target="tpu_custom_call" | custom-call | tf_op jit(solution)/shard_map/pallas_call | solution.py:391
  52.5 1.5 %copy.9 = bf16[256,128]{1,0:T(8,128)(2,1)} copy(bf16[256,128]{1,0:T(8,128)(2,1)} %shard_map.73) | data formatting | bytes 131072

commit v6 on v5

--- a/solution.py
+++ b/solution.py
@@ -71,10 +71,10 @@
 def kernel(
     nx, ny, nz,
     act, weight, down, up, home, served, var, out,
-    abuf, wmine, wother, ybuf, sel, xsend, xrelay, xrecv,
+    abuf, wmine, wother, ybuf, ubuf, sel, xsend, xrelay, xrecv, usend, urecv,
     acc, whole, parts, parts_in, shrunk, swap_in, table, homes, lists, var_row, var_wide,
     chooser, opener,
-    permuted, local_sem, z_recv, y_recv, relay_recv, sent, got, pair_send, pair_recv,
+    permuted, local_sem, z_recv, y_recv, u_recv, relay_recv, sent, got, pair_send, pair_recv,
 ):
     grp, tp = lax.axis_index("grp"), lax.axis_index("tp")
     x, y = grp // ny, lax.rem(grp, ny)
@@ -82,7 +82,6 @@
     tokens = out.shape[0]
     cols = out.shape[1]
     groups = nx * ny
-    blocks = down.shape[0]
     far = 1 - 2 * core
 
     def at_x(step):
@@ -99,9 +98,9 @@
     local = [
         pltpu.make_async_copy(home, homes, local_sem.at[4]),
         pltpu.make_async_copy(served, lists, local_sem.at[5]),
-        pltpu.make_async_copy(down, ybuf.at[0, pl.ds(0, blocks)], local_sem.at[1]),
+        pltpu.make_async_copy(down, ybuf.at[0], local_sem.at[1]),
         pltpu.make_async_copy(act, abuf.at[0], local_sem.at[0]),
-        pltpu.make_async_copy(up, ybuf.at[0, pl.ds(blocks, up.shape[0])], local_sem.at[2]),
+        pltpu.make_async_copy(up, ubuf.at[0], local_sem.at[2]),
         pltpu.make_async_copy(var, var_row, local_sem.at[6]),
         pltpu.make_async_copy(weight.at[:, core], wmine, local_sem.at[3]),
     ]
@@ -181,6 +180,7 @@
 
     zring = Ring(abuf, 2, (at_z(1), at_z(-1)), sent.at[0], z_recv)
     yring = Ring(ybuf, 4, (at_y(1), at_y(-1)), sent.at[1], y_recv)
+    uring = Ring(ubuf, 2, (at_y(1), at_y(-1)), sent.at[6], u_recv)
 
     def pair(index, src, dst):
         return pltpu.make_async_remote_copy(
@@ -189,7 +189,6 @@
         )
 
     local[2].wait()
-    local[4].wait()
     yring.start()
     local[3].wait()
     zring.start()
@@ -223,10 +222,8 @@
     def choose(number):
         first, count = groups_of_places[number]
         chunks = [chunk(first + k) for k in range(count)]
-        ups = [ybuf[d, pl.ds(blocks, up.shape[0])].reshape(up_rows, cols) for d in chunks]
-        chosen = jnp.dot(chooser[...], jnp.concatenate(ups, axis=1), preferred_element_type=F32).astype(BF16)
         for k in range(count):
-            sel[k] = ybuf[chunks[k], pl.ds(0, blocks)]
+            sel[k] = ybuf[chunks[k]]
         for e in (2, 1, 3, 0):
 
             def take(j):
@@ -239,14 +236,19 @@
 
             for j in range(SLOTS):
                 take(j)
-            for k in range(count):
-                rows = chosen[e * SLOTS * 4:(e + 1) * SLOTS * 4, k * cols:(k + 1) * cols].reshape(2, 16, cols)
-                if e == 0:
-                    xrecv[0, first + k, pl.ds(SLOTS, 2)] = rows
-                else:
-                    xsend[e, first + k, pl.ds(SLOTS, 2)] = rows
             if e:
                 hand(e, number).start()
+
+    def choose_up():
+        ups = [ubuf[chunk(place)].reshape(up_rows, cols) for place in range(ny)]
+        chosen = jnp.dot(chooser[...], jnp.concatenate(ups, axis=1), preferred_element_type=F32).astype(BF16)
+        for place in range(ny):
+            rows = chosen[:, place * cols:(place + 1) * cols].reshape(nx, 2, 16, cols)
+            for e in range(nx):
+                usend[e, place] = rows[e]
+
+    def hand_up(e):
+        return remote(usend.at[e], urecv.at[e], sent.at[7], got.at[0], at_x(e))
 
     def relay(number):
         if number != len(groups_of_places) - 1:
@@ -266,22 +268,28 @@
         loop(0, 2, add)
 
     z_events, y_events = (list(ring.events()) for ring in (zring, yring))
+    choose(0)
     set_up_choice()
-    choose(0)
     set_up()
 
     for number, (hop, index) in enumerate(y_events):
+        if index == 0 and hop < yring.half:
+            zring.advance(*z_events[hop - 1])
         yring.advance(hop, index)
         if number + 1 == len(y_events) or y_events[number + 1][0] > hop:
             choose(hop)
             relay(hop - 1)
             if hop == 1:
+                local[4].wait()
+                uring.start()
                 weights.start()
-        if hop > 1 and index == 1:
-            zring.advance(*z_events[hop - 2])
-    set_up_tokens()
+            else:
+                for event in uring.events():
+                    if event[0] == hop - 1:
+                        uring.advance(*event)
     for event in z_events[yring.half - 1:-3]:
         zring.advance(*event)
+    set_up_tokens()
 
     all_got(1, xrecv.at[pl.ds(1, nx - 1)])
     mine = permuted[...]
@@ -306,6 +314,12 @@
     loop(1, nz, lambda e: [scatter(e, side).start() for side in range(2)])
     scatter(0, 1).start()
     zring.advance(*z_events[-3])
+    for event in uring.events():
+        if event[0] == uring.half:
+            uring.advance(*event)
+    choose_up()
+    loop(1, nx, lambda e: hand_up(e).start())
+    urecv[0] = usend[0]
     set_up_last()
     local[6].wait()
     weights.wait_recv()
@@ -331,7 +345,10 @@
     all_sent(2, xsend.at[pl.ds(1, nx - 1)])
     all_sent(3, xrelay)
     all_sent(4, parts_in.at[pl.ds(1, 2 * nz - 1)])
+    all_sent(6, ubuf.at[pl.ds(0, ny - 1)])
+    all_sent(7, usend.at[pl.ds(1, nx - 1)])
     weights.wait_send()
+    all_got(0, urecv.at[pl.ds(1, nx - 1)])
     all_got(3, shrunk.at[pl.ds(0, 2 * nz - 1)])
     wide = groups * 16
     both = jnp.concatenate([shrunk[pl.ds(p * nz, nz)].reshape(tokens, rank) for p in range(PIECES)], axis=1)
@@ -341,7 +358,7 @@
     which = (lax.broadcasted_iota(jnp.int32, (1, wide), 1) >> 3) & 1
     for h in range(2):
         part = jnp.where(who == which + 2 * h, opened, 0.0).astype(BF16)
-        total += jnp.dot(part, xrecv[:, :, SLOTS + h].reshape(wide, cols), preferred_element_type=F32)
+        total += jnp.dot(part, urecv[:, :, h].reshape(wide, cols), preferred_element_type=F32)
     last.wait_recv()
     out[...] = (total + swap_in[...]).astype(BF16)
 
@@ -365,11 +382,14 @@
         pltpu.VMEM((nz, tokens, depth), BF16),
         pltpu.VMEM((nz, depth, cols), BF16),
         pltpu.VMEM((nz, depth, cols), BF16),
-        pltpu.VMEM((ny, blocks + up.shape[0], 16, rank), BF16),
+        pltpu.VMEM((ny,) + down.shape, BF16),
+        pltpu.VMEM((ny,) + up.shape, BF16),
         pltpu.VMEM((2,) + down.shape, BF16),
-        pltpu.VMEM((nx, ny, SLOTS + 2, 16, rank), BF16),
-        pltpu.VMEM((ny - 1, SLOTS + 2, 16, rank), BF16),
-        pltpu.VMEM((nx, ny, SLOTS + 2, 16, rank), BF16),
+        pltpu.VMEM((nx, ny, SLOTS, 16, rank), BF16),
+        pltpu.VMEM((ny - 1, SLOTS, 16, rank), BF16),
+        pltpu.VMEM((nx, ny, SLOTS, 16, rank), BF16),
+        pltpu.VMEM((nx, ny, 2, 16, cols), BF16),
+        pltpu.VMEM((nx, ny, 2, 16, cols), BF16),
         pltpu.VMEM((tokens, 2 * cols), F32),
         pltpu.VMEM((PIECES, nz, share, rank), F32),
         pltpu.VMEM((PIECES, nz, share, rank), BF16),
@@ -385,8 +405,8 @@
         pltpu.VMEM((PIECES * rank, groups * 16), BF16),
         pltpu.VMEM((tokens, depth), BF16),
         dma((7,)),
-        dma((2, nz // 2, 2)), dma((2, ny // 2, 4)), dma((ny // 2,)),
-        dma((6,)), dma((4,)), dma((2,)), dma((2,)),
+        dma((2, nz // 2, 2)), dma((2, ny // 2, 4)), dma((2, ny // 2, 2)), dma((ny // 2,)),
+        dma((8,)), dma((4,)), dma((2,)), dma((2,)),
     ]
     return pl.pallas_call(
         functools.partial(kernel, nx, ny, nz),

time: 54.1 us -> 51.6 us (0.954)
  Pallas kernels: 52.5 us -> 49.9 us
    pallas_call x1, Pallas kernels: 52.5 us -> 49.9 us  [on_device(): pl.pallas_call(functools.partial(kernel, nx, ny, nz), out_shape=jax.Shape...]
where the time goes in v6:
time: 51.6 us; the launch traced here: 51.4 us
  Pallas kernels  49.9 us (97%)
  local copies, waits for them, and re-layouts  1.47 us (3%)
    pallas_call x1, Pallas kernels, on_device(): pl.pallas_call(functools.partial(kernel, nx, ny, nz), out_shape=jax.Shape...  49.9 us
    unnamed x1, local copies, waits for them, and re-layouts  1.47 us

profile of v6, /device:TPU:1, one launch (start us, length us, event | category | flops | bytes accessed | tf_op | source)
XLA Modules:
  0.0 51.4 jit_solution(5212044676512385842)
XLA Ops:
  0.0 49.9 %shard_map.73 = bf16[256,128]{1,0:T(8,128)(2,1)} custom-call(bf16[256,512]{1,0:T(8,128)(2,1)} %act.1, bf16[8,2,512,128]{3,2,1,0:T(8,128)(2,1)} %bitcast.4, bf16[32,16,128]{2,1,0:T(8,128)(2,1)} %down.1, bf16[8,16,128]{2,1,0:T(8,128)(2,1)} %bitcast.5, s32[32]{0:T(128)} %home.1, s32[4,32]{1,0:T(4,128)} %bitcast.6, s32[1,256]{1,0:T(1,128)} %bitcast.7), custom_call_target="tpu_custom_call" | custom-call | tf_op jit(solution)/shard_map/pallas_call | solution.py:411
  49.9 1.5 %copy.9 = bf16[256,128]{1,0:T(8,128)(2,1)} copy(bf16[256,128]{1,0:T(8,128)(2,1)} %shard_map.73) | data formatting | bytes 131072

commit v7 on v6

--- a/solution.py
+++ b/solution.py
@@ -71,8 +71,8 @@
 def kernel(
     nx, ny, nz,
     act, weight, down, up, home, served, var, out,
-    abuf, wmine, wother, ybuf, ubuf, sel, xsend, xrelay, xrecv, usend, urecv,
-    acc, whole, parts, parts_in, shrunk, swap_in, table, homes, lists, var_row, var_wide,
+    abuf, wmine, wother, ybuf, ubuf, sel, xsend, xrelay, xrecv, usend, urecv, uother,
+    acc, sums, sums_in, whole, parts, parts_in, shrunk, swap_in, table, homes, lists, var_row, var_wide,
     chooser, opener,
     permuted, local_sem, z_recv, y_recv, u_recv, relay_recv, sent, got, pair_send, pair_recv,
 ):
@@ -90,8 +90,8 @@
     def at_y(step):
         return (x * ny + lax.rem(y + step + ny, ny), tp)
 
-    def at_z(step, side=0):
-        return (grp, lax.rem(z + step + nz, nz) * 2 + (core if side == 0 else 1 - core))
+    def at_z(step):
+        return (grp, lax.rem(z + step + nz, nz) * 2 + core)
 
     other = (grp, z * 2 + 1 - core)
 
@@ -116,7 +116,7 @@
     greet(at_y(1))
     greet(at_y(-1))
     loop(1, nx, lambda e: greet(at_x(e)))
-    loop(1, nz, lambda e: [greet(at_z(e, side)) for side in range(2)])
+    loop(1, nz, lambda e: greet(at_z(e)))
 
     local[0].wait()
     local[1].wait()
@@ -164,9 +164,9 @@
         for e in range(nx):
             columns, from_group = sources(e)
             width = ny * 16
-            row = lax.broadcasted_iota(jnp.int32, (PIECES * rank, width), 0)
-            column = lax.broadcasted_iota(jnp.int32, (PIECES * rank, width), 1)
-            hit = row == ((column >> 2) & 1) * rank + from_group * 4 + (column & 3)
+            row = lax.broadcasted_iota(jnp.int32, (rank, width), 0)
+            column = lax.broadcasted_iota(jnp.int32, (rank, width), 1)
+            hit = (row == from_group * 4 + (column & 3)) & (((column >> 2) & 1) == core)
             opener[:, columns] = hit.astype(F32).astype(BF16)
 
     def set_up_tokens():
@@ -176,9 +176,9 @@
             row = jnp.broadcast_to(var_row[:, pl.ds(i, size)], (cols, size))
             var_wide[pl.ds(i, size), :] = row.T
 
-    pl.semaphore_wait(barrier, nx + 2 * nz)
-
-    zring = Ring(abuf, 2, (at_z(1), at_z(-1)), sent.at[0], z_recv)
+    pl.semaphore_wait(barrier, nx + nz + 1)
+
+    zring = Ring(abuf, 4, (at_z(1), at_z(-1)), sent.at[0], z_recv)
     yring = Ring(ybuf, 4, (at_y(1), at_y(-1)), sent.at[1], y_recv)
     uring = Ring(ubuf, 2, (at_y(1), at_y(-1)), sent.at[6], u_recv)
 
@@ -262,6 +262,8 @@
         return jnp.dot(abuf[slot], both, preferred_element_type=F32)
 
     def multiply_pair(hop):
+        z_step(max(0, len(waiting) - sum(event[0] > hop for event in z_events)))
+
         def add(k):
             acc[...] += multiply(hop + k * (nz - 2 * hop))
 
@@ -272,13 +274,19 @@
     set_up_choice()
     set_up()
 
+    waiting = list(z_events)
+
+    def z_step(count):
+        for event in waiting[:count]:
+            zring.advance(*event)
+        del waiting[:count]
+
     for number, (hop, index) in enumerate(y_events):
-        if index == 0 and hop < yring.half:
-            zring.advance(*z_events[hop - 1])
         yring.advance(hop, index)
         if number + 1 == len(y_events) or y_events[number + 1][0] > hop:
             choose(hop)
             relay(hop - 1)
+            z_step(1)
             if hop == 1:
                 local[4].wait()
                 uring.start()
@@ -287,8 +295,9 @@
                 for event in uring.events():
                     if event[0] == hop - 1:
                         uring.advance(*event)
-    for event in z_events[yring.half - 1:-3]:
-        zring.advance(*event)
+        elif index == 1:
+            z_step(1)
+    z_step(2)
     set_up_tokens()
 
     all_got(1, xrecv.at[pl.ds(1, nx - 1)])
@@ -299,21 +308,23 @@
         factor = jnp.concatenate([xrecv[:, :, v * PIECES + p].reshape(depth, rank) for p in range(PIECES)], axis=1)
         total = jnp.where(who == v, jnp.dot(mine, factor, preferred_element_type=F32), total)
     for p in range(PIECES):
-        part = total[:, p * rank:(p + 1) * rank]
-        parts[p] = part.astype(BF16).reshape(nz, share, rank)
-        whole[p] = part.reshape(nz, share, rank)
-
-    def scatter(e, side):
-        source = parts.at[core if side == 0 else 1 - core, lax.rem(z + e, nz)]
-        return remote(source, parts_in.at[side * nz + e], sent.at[4], got.at[2], at_z(e, side))
-
-    def spread(e, side):
-        shard = shrunk.at[core * nz + z]
-        return remote(shard, shard, sent.at[5], got.at[3], at_z(e, side))
-
-    loop(1, nz, lambda e: [scatter(e, side).start() for side in range(2)])
-    scatter(0, 1).start()
-    zring.advance(*z_events[-3])
+        sums[p] = total[:, p * rank:(p + 1) * rank]
+    first = pair(1, sums.at[1 - core], sums_in)
+    first.start()
+    z_step(1)
+    first.wait_recv()
+    total = sums[core] + sums_in[...]
+    whole[...] = total.reshape(nz, share, rank)
+    parts[...] = total.astype(BF16).reshape(nz, share, rank)
+
+    def scatter(e):
+        return remote(parts.at[lax.rem(z + e, nz)], parts_in.at[e - 1], sent.at[4], got.at[2], at_z(e))
+
+    def spread(e):
+        return remote(shrunk.at[z], shrunk.at[z], sent.at[5], got.at[3], at_z(e))
+
+    loop(1, nz, lambda e: scatter(e).start())
+    z_step(1)
     for event in uring.events():
         if event[0] == uring.half:
             uring.advance(*event)
@@ -321,48 +332,49 @@
     loop(1, nx, lambda e: hand_up(e).start())
     urecv[0] = usend[0]
     set_up_last()
+    all_got(2, parts_in)
+    shrunk[z] = (whole[z] + jnp.sum(parts_in[...].astype(F32), axis=0)).astype(BF16)
+    loop(1, nz, lambda e: spread(e).start())
+    z_step(1)
     local[6].wait()
     weights.wait_recv()
     acc[...] = multiply(0)
     multiply_pair(1)
-    all_got(2, parts_in.at[pl.ds(1, 2 * nz - 1)])
-    others = jnp.sum(parts_in[pl.ds(1, 2 * nz - 1)].astype(F32), axis=0)
-    shrunk[core * nz + z] = (whole[core, z] + others).astype(BF16)
-    loop(1, nz, lambda e: [spread(e, side).start() for side in range(2)])
-    spread(0, 1).start()
+    all_got(0, urecv.at[pl.ds(1, nx - 1)])
+    ups = pair(2, urecv, uother)
+    ups.start()
     for hop in range(2, nz // 2 - 1):
         multiply_pair(hop)
-
-    zring.advance(*z_events[-2])
-    multiply_pair(nz // 2 - 1)
-    zring.advance(*z_events[-1])
-    acc[...] += multiply(nz // 2)
-    last = pair(1, acc.at[:, pl.ds(cols, cols)], swap_in)
-    last.start()
-
-    all_sent(0, abuf.at[pl.ds(0, nz - 1)])
-    all_sent(1, ybuf.at[pl.ds(0, ny - 1)])
-    all_sent(2, xsend.at[pl.ds(1, nx - 1)])
-    all_sent(3, xrelay)
-    all_sent(4, parts_in.at[pl.ds(1, 2 * nz - 1)])
-    all_sent(6, ubuf.at[pl.ds(0, ny - 1)])
-    all_sent(7, usend.at[pl.ds(1, nx - 1)])
-    weights.wait_send()
-    all_got(0, urecv.at[pl.ds(1, nx - 1)])
-    all_got(3, shrunk.at[pl.ds(0, 2 * nz - 1)])
+    ups.wait_recv()
+
+    all_got(3, shrunk.at[pl.ds(0, nz - 1)])
     wide = groups * 16
-    both = jnp.concatenate([shrunk[pl.ds(p * nz, nz)].reshape(tokens, rank) for p in range(PIECES)], axis=1)
-    opened = jnp.dot(both, opener[...], preferred_element_type=F32)
-    total = acc[:, pl.ds(0, cols)]
+    opened = jnp.dot(shrunk[...].reshape(tokens, rank), opener[...], preferred_element_type=F32)
     who = jnp.concatenate([var_wide[:, pl.ds(0, min(cols, wide))]] * max(wide // cols, 1), axis=1)
     which = (lax.broadcasted_iota(jnp.int32, (1, wide), 1) >> 3) & 1
     for h in range(2):
         part = jnp.where(who == which + 2 * h, opened, 0.0).astype(BF16)
-        total += jnp.dot(part, urecv[:, :, h].reshape(wide, cols), preferred_element_type=F32)
+        both = jnp.concatenate([side[:, :, h].reshape(wide, cols) for side in (urecv, uother)], axis=1)
+        acc[...] += jnp.dot(part, both, preferred_element_type=F32)
+
+    multiply_pair(nz // 2 - 1)
+    all_sent(1, ybuf.at[pl.ds(0, ny - 1)])
+    all_sent(2, xsend.at[pl.ds(1, nx - 1)])
+    all_sent(3, xrelay)
+    all_sent(4, parts_in)
+    all_sent(5, shrunk.at[pl.ds(0, nz - 1)])
+    all_sent(6, ubuf.at[pl.ds(0, ny - 1)])
+    all_sent(7, usend.at[pl.ds(1, nx - 1)])
+    weights.wait_send()
+    first.wait_send()
+    ups.wait_send()
+    z_step(len(waiting))
+    acc[...] += multiply(nz // 2)
+    last = pair(3, acc.at[:, pl.ds(cols, cols)], swap_in)
+    last.start()
+    all_sent(0, abuf.at[pl.ds(0, nz - 1)])
     last.wait_recv()
-    out[...] = (total + swap_in[...]).astype(BF16)
-
-    all_sent(5, shrunk.at[pl.ds(0, 2 * nz - 1)])
+    out[...] = (acc[:, pl.ds(0, cols)] + swap_in[...]).astype(BF16)
     last.wait_send()
 
 
@@ -390,11 +402,14 @@
         pltpu.VMEM((nx, ny, SLOTS, 16, rank), BF16),
         pltpu.VMEM((nx, ny, 2, 16, cols), BF16),
         pltpu.VMEM((nx, ny, 2, 16, cols), BF16),
+        pltpu.VMEM((nx, ny, 2, 16, cols), BF16),
         pltpu.VMEM((tokens, 2 * cols), F32),
-        pltpu.VMEM((PIECES, nz, share, rank), F32),
-        pltpu.VMEM((PIECES, nz, share, rank), BF16),
-        pltpu.VMEM((2 * nz, share, rank), BF16),
-        pltpu.VMEM((PIECES * nz, share, rank), BF16),
+        pltpu.VMEM((PIECES, tokens, rank), F32),
+        pltpu.VMEM((tokens, rank), F32),
+        pltpu.VMEM((nz, share, rank), F32),
+        pltpu.VMEM((nz, share, rank), BF16),
+        pltpu.VMEM((nz - 1, share, rank), BF16),
+        pltpu.VMEM((nz, share, rank), BF16),
         pltpu.VMEM((tokens, cols), F32),
         pltpu.SMEM((nx * SLOTS,), jnp.int32),
         pltpu.SMEM(home.shape, jnp.int32),
@@ -402,11 +417,11 @@
         pltpu.VMEM(var.shape, jnp.int32),
         pltpu.VMEM((tokens, cols), jnp.int32),
         pltpu.VMEM((nx * SLOTS * 4, blocks * 4), BF16),
-        pltpu.VMEM((PIECES * rank, groups * 16), BF16),
+        pltpu.VMEM((rank, groups * 16), BF16),
         pltpu.VMEM((tokens, depth), BF16),
         dma((7,)),
-        dma((2, nz // 2, 2)), dma((2, ny // 2, 4)), dma((2, ny // 2, 2)), dma((ny // 2,)),
-        dma((8,)), dma((4,)), dma((2,)), dma((2,)),
+        dma((2, nz // 2, 4)), dma((2, ny // 2, 4)), dma((2, ny // 2, 2)), dma((ny // 2,)),
+        dma((8,)), dma((4,)), dma((4,)), dma((4,)),
     ]
     return pl.pallas_call(
         functools.partial(kernel, nx, ny, nz),

time: 51.6 us -> 51.2 us (level)
  no operation moved by 1% of the time
where the time goes in v7:
time: 51.2 us; the launch traced here: 51 us
  Pallas kernels  49.5 us (97%)
  local copies, waits for them, and re-layouts  1.47 us (3%)
    pallas_call x1, Pallas kernels, on_device(): pl.pallas_call(functools.partial(kernel, nx, ny, nz), out_shape=jax.Shape...  49.5 us
    unnamed x1, local copies, waits for them, and re-layouts  1.47 us

profile of v7, /device:TPU:1, one launch (start us, length us, event | category | flops | bytes accessed | tf_op | source)
XLA Modules:
  0.0 51.0 jit_solution(9202674171207067602)
XLA Ops:
  0.0 49.5 %shard_map.73 = bf16[256,128]{1,0:T(8,128)(2,1)} custom-call(bf16[256,512]{1,0:T(8,128)(2,1)} %act.1, bf16[8,2,512,128]{3,2,1,0:T(8,128)(2,1)} %bitcast.4, bf16[32,16,128]{2,1,0:T(8,128)(2,1)} %down.1, bf16[8,16,128]{2,1,0:T(8,128)(2,1)} %bitcast.5, s32[32]{0:T(128)} %home.1, s32[4,32]{1,0:T(4,128)} %bitcast.6, s32[1,256]{1,0:T(1,128)} %bitcast.7), custom_call_target="tpu_custom_call" | custom-call | tf_op jit(solution)/shard_map/pallas_call | solution.py:426
  49.6 1.5 %copy.9 = bf16[256,128]{1,0:T(8,128)(2,1)} copy(bf16[256,128]{1,0:T(8,128)(2,1)} %shard_map.73) | data formatting | bytes 131072

commit v8 on v7

--- a/solution.py
+++ b/solution.py
@@ -74,7 +74,7 @@
     abuf, wmine, wother, ybuf, ubuf, sel, xsend, xrelay, xrecv, usend, urecv, uother,
     acc, sums, sums_in, whole, parts, parts_in, shrunk, swap_in, table, homes, lists, var_row, var_wide,
     chooser, opener,
-    permuted, local_sem, z_recv, y_recv, u_recv, relay_recv, sent, got, pair_send, pair_recv,
+    permuted, early, local_sem, z_recv, y_recv, u_recv, relay_recv, sent, got, pair_send, pair_recv,
 ):
     grp, tp = lax.axis_index("grp"), lax.axis_index("tp")
     x, y = grp // ny, lax.rem(grp, ny)
@@ -94,6 +94,17 @@
         return (grp, lax.rem(z + step + nz, nz) * 2 + core)
 
     other = (grp, z * 2 + 1 - core)
+
+    barrier = pltpu.get_barrier_semaphore()
+
+    def greet(partner):
+        pl.semaphore_signal(barrier, inc=1, device_id=partner, device_id_type=MESH)
+
+    greet(other)
+    greet(at_y(1))
+    greet(at_y(-1))
+    loop(1, nx, lambda e: greet(at_x(e)))
+    loop(1, nz, lambda e: greet(at_z(e)))
 
     local = [
         pltpu.make_async_copy(home, homes, local_sem.at[4]),
@@ -107,17 +118,6 @@
     for copy in local:
         copy.start()
 
-    barrier = pltpu.get_barrier_semaphore()
-
-    def greet(partner):
-        pl.semaphore_signal(barrier, inc=1, device_id=partner, device_id_type=MESH)
-
-    greet(other)
-    greet(at_y(1))
-    greet(at_y(-1))
-    loop(1, nx, lambda e: greet(at_x(e)))
-    loop(1, nz, lambda e: greet(at_z(e)))
-
     local[0].wait()
     local[1].wait()
 
@@ -151,14 +151,17 @@
         return pl.ds(e * width, width), lax.rem(x + nx - e, nx) * ny + ((y - behind_y) & (ny - 1))
 
     def set_up():
-        for e in range(nx):
-            columns, from_group = sources(e)
-            width = ny * 16
+        width = min(128, depth)
+        for at in range(0, depth, width):
+            column = lax.broadcasted_iota(jnp.int32, (1, width), 1) + at
+            place = column >> 6
+            e = (column >> 4) & (nx - 1)
+            behind_y = jnp.where((place & 1) == 1, (place + 1) >> 1, ny - (place >> 1))
+            from_group = ((x - e) & (nx - 1)) * ny + ((y - behind_y) & (ny - 1))
             row = lax.broadcasted_iota(jnp.int32, (depth, width), 0)
-            column = lax.broadcasted_iota(jnp.int32, (depth, width), 1)
             hit = row == from_group * 16 + (column & 15)
             moved = jnp.dot(abuf[0], hit.astype(F32).astype(BF16), preferred_element_type=F32)
-            permuted[:, columns] = moved.astype(BF16)
+            permuted[:, at:at + width] = moved.astype(BF16)
 
     def set_up_last():
         for e in range(nx):
@@ -213,11 +216,14 @@
     def chunk(place):
         return (place + 1) // 2 if place % 2 else (ny - place // 2) % ny
 
+    def turn(number):
+        return 1 if number < len(groups_of_places) - 2 else 4
+
     def hand(e, number):
         places = pl.ds(*groups_of_places[number])
         if e == 2 and number != len(groups_of_places) - 1:
             return remote(xsend.at[2, places], xrelay.at[places], sent.at[2], relay_recv.at[number], at_x(far))
-        return remote(xsend.at[e, places], xrecv.at[e, places], sent.at[2], got.at[1], at_x(e))
+        return remote(xsend.at[e, places], xrecv.at[places, e], sent.at[2], got.at[turn(number)], at_x(e))
 
     def choose(number):
         first, count = groups_of_places[number]
@@ -230,7 +236,7 @@
                 slot = table[e * SLOTS + j]
                 for k in range(count):
                     if e == 0:
-                        xrecv[0, first + k, j] = sel[k, slot]
+                        xrecv[first + k, 0, j] = sel[k, slot]
                     else:
                         xsend[e, first + k, j] = sel[k, slot]
 
@@ -254,7 +260,7 @@
         if number != len(groups_of_places) - 1:
             hand(2, number).wait_recv()
             places = pl.ds(*groups_of_places[number])
-            remote(xrelay.at[places], xrecv.at[2, places], sent.at[3], got.at[1], at_x(far)).start()
+            remote(xrelay.at[places], xrecv.at[places, 2], sent.at[3], got.at[turn(number)], at_x(far)).start()
 
     def multiply(slot):
         place = lax.rem(z - slot + nz, nz)
@@ -273,6 +279,11 @@
     choose(0)
     set_up_choice()
     set_up()
+
+    def u_step(hop):
+        for event in uring.events():
+            if event[0] == hop and hop > 0:
+                uring.advance(*event)
 
     waiting = list(z_events)
 
@@ -288,30 +299,42 @@
             relay(hop - 1)
             z_step(1)
             if hop == 1:
+                weights.start()
+            if hop == min(2, yring.half):
                 local[4].wait()
                 uring.start()
-                weights.start()
-            else:
-                for event in uring.events():
-                    if event[0] == hop - 1:
-                        uring.advance(*event)
+            u_step(hop - 2)
         elif index == 1:
             z_step(1)
     z_step(2)
     set_up_tokens()
 
-    all_got(1, xrecv.at[pl.ds(1, nx - 1)])
-    mine = permuted[...]
-    total = jnp.zeros((tokens, PIECES * rank), F32)
+    cut = groups_of_places[-2][0] if ny > 2 else 0
     who = jnp.concatenate([var_wide[:, pl.ds(0, rank)]] * PIECES, axis=1)
-    for v in range(VPG):
-        factor = jnp.concatenate([xrecv[:, :, v * PIECES + p].reshape(depth, rank) for p in range(PIECES)], axis=1)
-        total = jnp.where(who == v, jnp.dot(mine, factor, preferred_element_type=F32), total)
+
+    def shrink(first, end):
+        mine = permuted[:, first * nx * 16:end * nx * 16]
+        total = jnp.zeros((tokens, PIECES * rank), F32)
+        for v in range(VPG):
+            slots = [xrecv[first:end, :, v * PIECES + p].reshape(-1, rank) for p in range(PIECES)]
+            product = jnp.dot(mine, jnp.concatenate(slots, axis=1), preferred_element_type=F32)
+            total = jnp.where(who == v, product, total)
+        return total
+
+    if cut:
+        all_got(1, xrecv.at[pl.ds(0, cut), pl.ds(1, nx - 1)])
+        early[...] = shrink(0, cut)
+    all_got(4, xrecv.at[pl.ds(cut, ny - cut), pl.ds(1, nx - 1)])
+    total = shrink(cut, ny)
+    if cut:
+        total += early[...]
     for p in range(PIECES):
         sums[p] = total[:, p * rank:(p + 1) * rank]
     first = pair(1, sums.at[1 - core], sums_in)
     first.start()
     z_step(1)
+    if uring.half > 1:
+        u_step(uring.half - 1)
     first.wait_recv()
     total = sums[core] + sums_in[...]
     whole[...] = total.reshape(nz, share, rank)
@@ -325,9 +348,7 @@
 
     loop(1, nz, lambda e: scatter(e).start())
     z_step(1)
-    for event in uring.events():
-        if event[0] == uring.half:
-            uring.advance(*event)
+    u_step(uring.half)
     choose_up()
     loop(1, nx, lambda e: hand_up(e).start())
     urecv[0] = usend[0]
@@ -343,7 +364,7 @@
     all_got(0, urecv.at[pl.ds(1, nx - 1)])
     ups = pair(2, urecv, uother)
     ups.start()
-    for hop in range(2, nz // 2 - 1):
+    for hop in range(2, min(3, nz // 2)):
         multiply_pair(hop)
     ups.wait_recv()
 
@@ -357,7 +378,8 @@
         both = jnp.concatenate([side[:, :, h].reshape(wide, cols) for side in (urecv, uother)], axis=1)
         acc[...] += jnp.dot(part, both, preferred_element_type=F32)
 
-    multiply_pair(nz // 2 - 1)
+    for hop in range(3, nz // 2):
+        multiply_pair(hop)
     all_sent(1, ybuf.at[pl.ds(0, ny - 1)])
     all_sent(2, xsend.at[pl.ds(1, nx - 1)])
     all_sent(3, xrelay)
@@ -399,7 +421,7 @@
         pltpu.VMEM((2,) + down.shape, BF16),
         pltpu.VMEM((nx, ny, SLOTS, 16, rank), BF16),
         pltpu.VMEM((ny - 1, SLOTS, 16, rank), BF16),
-        pltpu.VMEM((nx, ny, SLOTS, 16, rank), BF16),
+        pltpu.VMEM((ny, nx, SLOTS, 16, rank), BF16),
         pltpu.VMEM((nx, ny, 2, 16, cols), BF16),
         pltpu.VMEM((nx, ny, 2, 16, cols), BF16),
         pltpu.VMEM((nx, ny, 2, 16, cols), BF16),
@@ -419,9 +441,10 @@
         pltpu.VMEM((nx * SLOTS * 4, blocks * 4), BF16),
         pltpu.VMEM((rank, groups * 16), BF16),
         pltpu.VMEM((tokens, depth), BF16),
+        pltpu.VMEM((tokens, PIECES * rank), F32),
         dma((7,)),
         dma((2, nz // 2, 4)), dma((2, ny // 2, 4)), dma((2, ny // 2, 2)), dma((ny // 2,)),
-        dma((8,)), dma((4,)), dma((4,)), dma((4,)),
+        dma((8,)), dma((5,)), dma((4,)), dma((4,)),
     ]
     return pl.pallas_call(
         functools.partial(kernel, nx, ny, nz),

time: 51.2 us -> 50.8 us (level)
  no operation moved by 1% of the time
where the time goes in v8:
time: 50.8 us; the launch traced here: 50.6 us
  Pallas kernels  49.2 us (97%)
  local copies, waits for them, and re-layouts  1.47 us (3%)
    pallas_call x1, Pallas kernels, on_device(): pl.pallas_call(functools.partial(kernel, nx, ny, nz), out_shape=jax.Shape...  49.2 us
    unnamed x1, local copies, waits for them, and re-layouts  1.47 us

profile of v8, /device:TPU:1, one launch (start us, length us, event | category | flops | bytes accessed | tf_op | source)
XLA Modules:
  0.0 50.6 jit_solution(5502180692908102298)
XLA Ops:
  0.0 49.2 %shard_map.73 = bf16[256,128]{1,0:T(8,128)(2,1)} custom-call(bf16[256,512]{1,0:T(8,128)(2,1)} %act.1, bf16[8,2,512,128]{3,2,1,0:T(8,128)(2,1)} %bitcast.4, bf16[32,16,128]{2,1,0:T(8,128)(2,1)} %down.1, bf16[8,16,128]{2,1,0:T(8,128)(2,1)} %bitcast.5, s32[32]{0:T(128)} %home.1, s32[4,32]{1,0:T(4,128)} %bitcast.6, s32[1,256]{1,0:T(1,128)} %bitcast.7), custom_call_target="tpu_custom_call" | custom-call | tf_op jit(solution)/shard_map/pallas_call | solution.py:449
  49.2 1.5 %copy.9 = bf16[256,128]{1,0:T(8,128)(2,1)} copy(bf16[256,128]{1,0:T(8,128)(2,1)} %shard_map.73) | data formatting | bytes 131072

commit v9 on v8

--- a/solution.py
+++ b/solution.py
@@ -16,8 +16,8 @@
 
 
 class Ring:
-    def __init__(self, buf, pieces, peers, send, recv):
-        self.buf, self.pieces, self.peers = buf, pieces, peers
+    def __init__(self, own, buf, pieces, peers, send, recv):
+        self.own, self.buf, self.pieces, self.peers = own, buf, pieces, peers
         self.send, self.recv = send, recv
         self.n = buf.shape[0]
         self.half = self.n // 2
@@ -40,7 +40,7 @@
     def copy(self, way, hop, index):
         cut = self.cut(way, index)
         return pltpu.make_async_remote_copy(
-            src_ref=self.buf.at[self.slot(way, hop - 1), cut],
+            src_ref=self.own.at[cut] if hop == 1 else self.buf.at[self.slot(way, hop - 1), cut],
             dst_ref=self.buf.at[self.slot(way, hop), cut],
             send_sem=self.send,
             recv_sem=self.recv.at[way, hop - 1, index],
@@ -118,16 +118,6 @@
     for copy in local:
         copy.start()
 
-    local[0].wait()
-    local[1].wait()
-
-    def fill(k, carry):
-        owner = lax.rem(x + k // SLOTS, nx) * ny + y
-        j = lax.rem(k, SLOTS)
-        table[k] = homes[lists[j // PIECES, owner] * PIECES + lax.rem(j, PIECES)]
-        return carry
-
-    lax.fori_loop(0, nx * SLOTS, fill, 0)
     up_rows = up.shape[0] * up.shape[1]
     rank = xrecv.shape[-1]
     depth = act.shape[1]
@@ -181,9 +171,9 @@
 
     pl.semaphore_wait(barrier, nx + nz + 1)
 
-    zring = Ring(abuf, 4, (at_z(1), at_z(-1)), sent.at[0], z_recv)
-    yring = Ring(ybuf, 4, (at_y(1), at_y(-1)), sent.at[1], y_recv)
-    uring = Ring(ubuf, 2, (at_y(1), at_y(-1)), sent.at[6], u_recv)
+    zring = Ring(act, abuf, 4, (at_z(1), at_z(-1)), sent.at[0], z_recv)
+    yring = Ring(down, ybuf, 4, (at_y(1), at_y(-1)), sent.at[1], y_recv)
+    uring = Ring(up, ubuf, 2, (at_y(1), at_y(-1)), sent.at[6], u_recv)
 
     def pair(index, src, dst):
         return pltpu.make_async_remote_copy(
@@ -191,10 +181,18 @@
             device_id=other, device_id_type=MESH,
         )
 
-    local[2].wait()
     yring.start()
-    local[3].wait()
     zring.start()
+    local[0].wait()
+    local[1].wait()
+
+    def fill(k, carry):
+        owner = lax.rem(x + k // SLOTS, nx) * ny + y
+        j = lax.rem(k, SLOTS)
+        table[k] = homes[lists[j // PIECES, owner] * PIECES + lax.rem(j, PIECES)]
+        return carry
+
+    lax.fori_loop(0, nx * SLOTS, fill, 0)
     weights = pair(0, weight.at[:, 1 - core], wother)
 
     def behind(d):
@@ -276,8 +274,10 @@
         loop(0, 2, add)
 
     z_events, y_events = (list(ring.events()) for ring in (zring, yring))
+    local[2].wait()
     choose(0)
     set_up_choice()
+    local[3].wait()
     set_up()
 
     def u_step(hop):
@@ -301,7 +301,6 @@
             if hop == 1:
                 weights.start()
             if hop == min(2, yring.half):
-                local[4].wait()
                 uring.start()
             u_step(hop - 2)
         elif index == 1:
@@ -324,6 +323,7 @@
     if cut:
         all_got(1, xrecv.at[pl.ds(0, cut), pl.ds(1, nx - 1)])
         early[...] = shrink(0, cut)
+    z_step(1)
     all_got(4, xrecv.at[pl.ds(cut, ny - cut), pl.ds(1, nx - 1)])
     total = shrink(cut, ny)
     if cut:
@@ -332,7 +332,6 @@
         sums[p] = total[:, p * rank:(p + 1) * rank]
     first = pair(1, sums.at[1 - core], sums_in)
     first.start()
-    z_step(1)
     if uring.half > 1:
         u_step(uring.half - 1)
     first.wait_recv()
@@ -349,6 +348,7 @@
     loop(1, nz, lambda e: scatter(e).start())
     z_step(1)
     u_step(uring.half)
+    local[4].wait()
     choose_up()
     loop(1, nx, lambda e: hand_up(e).start())
     urecv[0] = usend[0]

time: 50.8 us -> 50.8 us (level)
  no operation moved by 1% of the time
where the time goes in v9:
time: 50.8 us; the launch traced here: 50.6 us
  Pallas kernels  49.2 us (97%)
  local copies, waits for them, and re-layouts  1.47 us (3%)
    pallas_call x1, Pallas kernels, on_device(): pl.pallas_call(functools.partial(kernel, nx, ny, nz), out_shape=jax.Shape...  49.2 us
    unnamed x1, local copies, waits for them, and re-layouts  1.47 us

profile of v9, /device:TPU:1, one launch (start us, length us, event | category | flops | bytes accessed | tf_op | source)
XLA Modules:
  0.0 50.6 jit_solution(14913714270940560610)
XLA Ops:
  0.0 49.2 %shard_map.73 = bf16[256,128]{1,0:T(8,128)(2,1)} custom-call(bf16[256,512]{1,0:T(8,128)(2,1)} %act.1, bf16[8,2,512,128]{3,2,1,0:T(8,128)(2,1)} %bitcast.4, bf16[32,16,128]{2,1,0:T(8,128)(2,1)} %down.1, bf16[8,16,128]{2,1,0:T(8,128)(2,1)} %bitcast.5, s32[32]{0:T(128)} %home.1, s32[4,32]{1,0:T(4,128)} %bitcast.6, s32[1,256]{1,0:T(1,128)} %bitcast.7), custom_call_target="tpu_custom_call" | custom-call | tf_op jit(solution)/shard_map/pallas_call | solution.py:449
  49.2 1.5 %copy.9 = bf16[256,128]{1,0:T(8,128)(2,1)} copy(bf16[256,128]{1,0:T(8,128)(2,1)} %shard_map.73) | data formatting | bytes 131072

commit v10 on v9

--- a/solution.py
+++ b/solution.py
@@ -115,7 +115,7 @@
         pltpu.make_async_copy(var, var_row, local_sem.at[6]),
         pltpu.make_async_copy(weight.at[:, core], wmine, local_sem.at[3]),
     ]
-    for copy in local:
+    for copy in local[:-1]:
         copy.start()
 
     up_rows = up.shape[0] * up.shape[1]
@@ -298,13 +298,13 @@
             choose(hop)
             relay(hop - 1)
             z_step(1)
-            if hop == 1:
-                weights.start()
             if hop == min(2, yring.half):
                 uring.start()
             u_step(hop - 2)
         elif index == 1:
             z_step(1)
+    weights.start()
+    local[6].start()
     z_step(2)
     set_up_tokens()
 

time: 50.8 us -> 50.8 us (level)
  no operation moved by 1% of the time
where the time goes in v10:
time: 50.8 us; the launch traced here: 50.6 us
  Pallas kernels  49.2 us (97%)
  local copies, waits for them, and re-layouts  1.47 us (3%)
    pallas_call x1, Pallas kernels, on_device(): pl.pallas_call(functools.partial(kernel, nx, ny, nz), out_shape=jax.Shape...  49.2 us
    unnamed x1, local copies, waits for them, and re-layouts  1.47 us

profile of v10, /device:TPU:1, one launch (start us, length us, event | category | flops | bytes accessed | tf_op | source)
XLA Modules:
  0.0 50.6 jit_solution(153938283579206382)
XLA Ops:
  0.0 49.2 %shard_map.73 = bf16[256,128]{1,0:T(8,128)(2,1)} custom-call(bf16[256,512]{1,0:T(8,128)(2,1)} %act.1, bf16[8,2,512,128]{3,2,1,0:T(8,128)(2,1)} %bitcast.4, bf16[32,16,128]{2,1,0:T(8,128)(2,1)} %down.1, bf16[8,16,128]{2,1,0:T(8,128)(2,1)} %bitcast.5, s32[32]{0:T(128)} %home.1, s32[4,32]{1,0:T(4,128)} %bitcast.6, s32[1,256]{1,0:T(1,128)} %bitcast.7), custom_call_target="tpu_custom_call" | custom-call | tf_op jit(solution)/shard_map/pallas_call | solution.py:449
  49.2 1.5 %copy.9 = bf16[256,128]{1,0:T(8,128)(2,1)} copy(bf16[256,128]{1,0:T(8,128)(2,1)} %shard_map.73) | data formatting | bytes 131072

commit v11 on v10

--- a/solution.py
+++ b/solution.py
@@ -324,6 +324,7 @@
         all_got(1, xrecv.at[pl.ds(0, cut), pl.ds(1, nx - 1)])
         early[...] = shrink(0, cut)
     z_step(1)
+    u_step(uring.half - 1)
     all_got(4, xrecv.at[pl.ds(cut, ny - cut), pl.ds(1, nx - 1)])
     total = shrink(cut, ny)
     if cut:
@@ -332,26 +333,24 @@
         sums[p] = total[:, p * rank:(p + 1) * rank]
     first = pair(1, sums.at[1 - core], sums_in)
     first.start()
-    if uring.half > 1:
-        u_step(uring.half - 1)
-    first.wait_recv()
-    total = sums[core] + sums_in[...]
-    whole[...] = total.reshape(nz, share, rank)
-    parts[...] = total.astype(BF16).reshape(nz, share, rank)
-
-    def scatter(e):
-        return remote(parts.at[lax.rem(z + e, nz)], parts_in.at[e - 1], sent.at[4], got.at[2], at_z(e))
-
-    def spread(e):
-        return remote(shrunk.at[z], shrunk.at[z], sent.at[5], got.at[3], at_z(e))
-
-    loop(1, nz, lambda e: scatter(e).start())
-    z_step(1)
     u_step(uring.half)
     local[4].wait()
     choose_up()
     loop(1, nx, lambda e: hand_up(e).start())
     urecv[0] = usend[0]
+    first.wait_recv()
+    total = sums[core] + sums_in[...]
+    whole[...] = total.reshape(nz, share, rank)
+    parts[...] = total.astype(BF16).reshape(nz, share, rank)
+
+    def scatter(e):
+        return remote(parts.at[lax.rem(z + e, nz)], parts_in.at[e - 1], sent.at[4], got.at[2], at_z(e))
+
+    def spread(e):
+        return remote(shrunk.at[z], shrunk.at[z], sent.at[5], got.at[3], at_z(e))
+
+    loop(1, nz, lambda e: scatter(e).start())
+    z_step(1)
     set_up_last()
     all_got(2, parts_in)
     shrunk[z] = (whole[z] + jnp.sum(parts_in[...].astype(F32), axis=0)).astype(BF16)

time: 50.8 us -> 53 us (1.043)
  Pallas kernels: 49.2 us -> 51.4 us
    pallas_call x1, Pallas kernels: 49.2 us -> 51.4 us  [on_device(): pl.pallas_call(functools.partial(kernel, nx, ny, nz), out_shape=jax.Shape...]
where the time goes in v11:
time: 53 us; the launch traced here: 52.8 us
  Pallas kernels  51.4 us (97%)
  local copies, waits for them, and re-layouts  1.47 us (3%)
    pallas_call x1, Pallas kernels, on_device(): pl.pallas_call(functools.partial(kernel, nx, ny, nz), out_shape=jax.Shape...  51.4 us
    unnamed x1, local copies, waits for them, and re-layouts  1.47 us

profile of v11, /device:TPU:1, one launch (start us, length us, event | category | flops | bytes accessed | tf_op | source)
XLA Modules:
  0.0 52.8 jit_solution(9442752231792710148)
XLA Ops:
  0.0 51.4 %shard_map.73 = bf16[256,128]{1,0:T(8,128)(2,1)} custom-call(bf16[256,512]{1,0:T(8,128)(2,1)} %act.1, bf16[8,2,512,128]{3,2,1,0:T(8,128)(2,1)} %bitcast.4, bf16[32,16,128]{2,1,0:T(8,128)(2,1)} %down.1, bf16[8,16,128]{2,1,0:T(8,128)(2,1)} %bitcast.5, s32[32]{0:T(128)} %home.1, s32[4,32]{1,0:T(4,128)} %bitcast.6, s32[1,256]{1,0:T(1,128)} %bitcast.7), custom_call_target="tpu_custom_call" | custom-call | tf_op jit(solution)/shard_map/pallas_call | solution.py:448
  51.4 1.5 %copy.9 = bf16[256,128]{1,0:T(8,128)(2,1)} copy(bf16[256,128]{1,0:T(8,128)(2,1)} %shard_map.73) | data formatting | bytes 131072
